TPU v7x, 256 devices: a whole 4x4x8 slice. The times are simulated.
256 devices in a mesh: cache: 16 (over x, y), proj: 16 (over z, core).
Axes of the slice: x: 4, y: 4, z: 8, core: 2. Of those that a mesh axis runs over, the one named last changes fastest.
Arguments:
- compressed_query: bfloat16 [128, 1536], replicated, may hold values from -6 to 6
- query_gain: float32 [1536], replicated, may hold values from 0.25 to 1.75
- w_query: bfloat16 [1536, 24576], P('cache', 'proj'), may hold values from -0.15625 to 0.15625
- w_key: bfloat16 [128, 128, 512], P('proj'), may hold values from -0.5 to 0.5
- value_up_weight: bfloat16 [128, 512, 128], P('proj'), may hold values from -0.25 to 0.25
- w_output: bfloat16 [16384, 7168], P('proj', 'cache'), may hold values from -0.046875 to 0.046875
- latent_cache: bfloat16 [128, 16384, 576], P('proj', 'cache'), may hold values from -700 to 700
- context_lengths: int32 [128], replicated, may hold values from 8192 to 16384
- block_ids: int32 [128, 32], P('proj'), may hold values from -1 to 255, as said below
- block_counts: int32 [128], P('proj'), may hold values from 8 to 32
Outputs:
- attention_out: bfloat16 [128, 7168], P('proj', 'cache')
Inputs may be any that keep to these rules, and one draw needn't show every extreme that they name: `block_ids`: the first block_counts[r] entries of row r are distinct blocks of 64 positions that start before context_lengths[r], the first of them holding position context_lengths[r] - 1; the other entries are -1. At most 4 listed blocks of a row lie within one run of 1024 positions that starts at a multiple of 1024, and some row has exactly 4 in one such run.
All inputs are finite; a program needn't handle non-finite values.
Results may differ from a plain program's by a relative error of at most 0.027.
The roundings to bfloat16 on the way count: a program that leaves them out, or rounds other values in their place, can miss the bound.
Values may be sent and summed in bfloat16 or wider, within the bound.
A program may use at most 128 MiB of HBM per device.

v0:
```python
import jax
import jax.numpy as jnp
from jax import lax
from jax.sharding import PartitionSpec as P

NOPE = 128
ROPE = 64
KVR = 512
NSEL = 32
BLK = 64


def rotate(part, positions):
    half = part.shape[-1] // 2
    freq = 10000.0 ** (-(jnp.arange(half, dtype=jnp.float32) * 2.0 / part.shape[-1]))
    angle = positions.astype(jnp.float32)[:, None] * freq[None, :]
    cosine = jnp.cos(angle)[:, None, :]
    sine = jnp.sin(angle)[:, None, :]
    first = part[..., :half]
    second = part[..., half:]
    return jnp.concatenate([first * cosine - second * sine, first * sine + second * cosine], -1)


def absorb(query, positions, w_key):
    count = query.shape[0]
    heads = w_key.shape[0]
    query = query.reshape(count, heads, NOPE + ROPE)
    query_nope = query[..., :NOPE].astype(jnp.bfloat16)
    query_rope = rotate(query[..., NOPE:], positions - 1).astype(jnp.bfloat16)
    latent = jnp.einsum(
        "rhn,hnk->rhk", query_nope, w_key, preferred_element_type=jnp.float32
    ).astype(jnp.bfloat16)
    return (latent, query_rope)


def on_device(
    compressed_query,
    query_gain,
    w_query,
    w_key,
    value_up_weight,
    w_output,
    latent_cache,
    context_lengths,
    block_ids,
    block_counts,
):
    cache_rank = lax.axis_index("cache")
    proj_rank = lax.axis_index("proj")
    all_rows = compressed_query.shape[0]
    local_rows = latent_cache.shape[0]
    ctx_local = latent_cache.shape[1]
    ordinal_within = w_query.shape[0]
    source = compressed_query.astype(jnp.float32)
    normed = (
        source * lax.rsqrt(jnp.mean(source * source, -1, keepdims=True) + 1e-06) * query_gain
    ).astype(jnp.bfloat16)
    columns = lax.dynamic_slice_in_dim(normed, cache_rank * ordinal_within, ordinal_within, 1)
    partial_query = jnp.dot(columns, w_query, preferred_element_type=jnp.float32)
    query = lax.psum(partial_query, "cache")
    latent, query_rope = absorb(query, context_lengths, w_key)
    owned_latent, owned_rope = (
        lax.all_to_all(latent, "proj", split_axis=0, concat_axis=1, tiled=True),
        lax.all_to_all(query_rope, "proj", split_axis=0, concat_axis=1, tiled=True),
    )
    full_query = jnp.concatenate([owned_latent, owned_rope], -1)
    row_lengths = lax.dynamic_slice_in_dim(context_lengths, proj_rank * local_rows, local_rows, 0)
    blocks_local = ctx_local // BLK
    capacity = max(2, 2 * NSEL // lax.axis_size("cache"))
    first_block = cache_rank * blocks_local
    slot_live = jnp.arange(block_ids.shape[1], dtype=jnp.int32)[None, :] < block_counts[:, None]
    mine = slot_live & (block_ids >= first_block) & (block_ids < first_block + blocks_local)
    order = jnp.cumsum(mine.astype(jnp.int32), axis=1) - 1
    slot_table = mine[:, :, None] & (
        order[:, :, None] == jnp.arange(capacity, dtype=jnp.int32)[None, None, :]
    )
    filled = jnp.any(slot_table, axis=1)
    local_block = jnp.sum(jnp.where(slot_table, (block_ids - first_block)[:, :, None], 0), axis=1)
    offsets = (
        local_block[:, :, None] * BLK + jnp.arange(BLK, dtype=jnp.int32)[None, None, :]
    ).reshape(local_rows, capacity * BLK)
    keys = jnp.take_along_axis(latent_cache, offsets[:, :, None], axis=1)
    position = cache_rank * ctx_local + offsets
    token_filled = jnp.broadcast_to(filled[:, :, None], (local_rows, capacity, BLK)).reshape(
        local_rows, capacity * BLK
    )
    live = token_filled & (position < row_lengths[:, None])
    scale = (NOPE + ROPE) ** (-0.5)
    scores = (
        jnp.einsum("rhk,rtk->rht", full_query, keys, preferred_element_type=jnp.float32) * scale
    )
    largest = jnp.max(jnp.where(live[:, None, :], scores, -1e30), -1)
    top = lax.pmax(largest, "cache")
    weights = jnp.where(live[:, None, :], jnp.exp(scores - top[..., None]), 0.0)
    total = jnp.sum(weights, -1)
    summed = jnp.einsum(
        "rht,rtk->rhk",
        weights.astype(jnp.bfloat16),
        keys[..., :KVR],
        preferred_element_type=jnp.float32,
    )
    whole_total, whole_sum = lax.psum((total, summed), "cache")
    attended_latent_rows = (whole_sum / whole_total[..., None]).astype(jnp.bfloat16)
    per_head_output = lax.all_to_all(
        attended_latent_rows, "proj", split_axis=1, concat_axis=0, tiled=True
    )
    value_rows = jnp.einsum(
        "sat,atl->sal", per_head_output, value_up_weight, preferred_element_type=jnp.float32
    ).astype(jnp.bfloat16)
    flat_values = value_rows.reshape(all_rows, -1)
    output = lax.psum_scatter(
        jnp.dot(flat_values, w_output, preferred_element_type=jnp.float32),
        "proj",
        scatter_dimension=0,
        tiled=True,
    )
    return output.astype(jnp.bfloat16)


def solution(mesh):
    placed = (
        P(),
        P(),
        P("cache", "proj"),
        P("proj", None, None),
        P("proj", None, None),
        P("proj", "cache"),
        P("proj", "cache", None),
        P(),
        P("proj", None),
        P("proj"),
    )
    return jax.shard_map(
        on_device, mesh=mesh, in_specs=placed, out_specs=P("proj", "cache"), check_vma=False
    )
```

profile of v0, /device:TPU:1, one launch (start us, length us, event | category | flops | bytes accessed | tf_op | source)
XLA Modules:
  0.0 432.7 jit_solution(17044360453520946900)
XLA Ops:
  6.5 1.2 convert_element_type.36
  7.7 0.0 copy-start.6
  7.7 1.2 multiply_reduce_fusion
  8.9 0.8 dynamic-slice
  9.7 1.3 fusion.16
  11.0 1.4 copy.56
  12.4 0.0 all-reduce.3.cloned.1.call-update
  12.4 0.0 copy-done.6
  12.4 0.3 multiply_cosine_fusion
  12.7 99.3 %all-reduce.3.cloned.1.call-done = f32[128,8,192]{2,0,1:T(8,128)} async-done(((f32[128,8,192]{2,0,1:T(8,128)}), f32[128,8,192]{2,0,1:T(8,128)}) %all-reduce.3.cloned.1.call-update) | async-done | bytes 786448 | tf_op jit(solution)/shard_map/psum | solution.py:60
  112.0 1.5 subtract_convert_fusion
  113.5 0.1 pad_maximum_fusion
  113.7 0.2 copy.59
  113.9 0.9 reshape.237
  114.8 9.2 %all-to-all-start.1 = ((bf16[16,2,2048]{2,1,0:T(2,128)(2,1)}), bf16[16,2,2048]{2,1,0:T(2,128)(2,1)S(1)}, u32[]{:S(2)}, u32[]{:S(2)}) async-start(bf16[16,2,2048]{2,1,0:T(2,128)(2,1)} %reshape.237), calls=%async_computation.1 | async-start | bytes 262144 | tf_op jit(solution)/shard_map/all_to_all | solution.py:64
  124.0 0.0 copy-done.1
  124.0 0.4 fusion.2
  124.4 0.0 copy-start.4
  124.4 0.0 copy-start.5
  124.4 1.6 copy.57
  126.0 7.1 %all-to-all-done.1 = bf16[16,2,2048]{2,1,0:T(2,128)(2,1)S(1)} async-done(((bf16[16,2,2048]{2,1,0:T(2,128)(2,1)}), bf16[16,2,2048]{2,1,0:T(2,128)(2,1)S(1)}, u32[]{:S(2)}, u32[]{:S(2)}) %all-to-all-start.1) | async-done | bytes 131104 | tf_op jit(solution)/shard_map/all_to_all | solution.py:64
  133.1 3.6 all-to-all-start
  136.7 0.0 all-reduce.5.cloned.1.call-start
  136.8 0.1 fusion.32
  136.9 0.2 reduce_window_sum.11
  137.0 0.1 select_reduce_fusion.1
  137.2 0.1 copy.54
  137.3 0.1 add.123
  137.4 0.1 add.124
  137.4 0.1 add.137
  137.5 0.2 fusion.21
  137.7 0.1 copy.53
  137.8 0.1 broadcast_in_dim.40
  137.9 0.1 reshape.228
  138.0 0.1 dynamic_slice.6
  138.0 0.1 add.126
  138.2 14.1 %copy.63 = bf16[8,1024,576]{2,1,0:T(8,128)(2,1)} copy(bf16[8,1024,576]{1,2,0:T(8,128)(2,1)} %param.16) | data formatting | bytes 18874368 | tf_op args[6]
  152.3 38.4 %gather_fusion = bf16[2048,576]{1,0:T(8,128)(2,1)} fusion(bf16[8,1024,576]{2,1,0:T(8,128)(2,1)} %copy.63, s32[2048]{0:T(1024)S(1)} %bitcast.35), kind=kCustom, calls=%fused_computation | custom fusion | bytes 4734976 | tf_op jit(solution)/shard_map/jit(take_along_axis)/gather | solution.py:82
  190.7 0.1 fusion.26
  190.7 3.1 broadcast_select_fusion
  193.8 0.2 reshape.238
  194.1 0.1 copy.62
  194.2 0.0 all-to-all-done
  194.2 0.1 copy.78
  194.3 1.3 copy.61
  195.6 3.1 select_reduce_fusion
  198.8 30.9 %pmax.7 = f32[8,128]{1,0:T(8,128)S(1)} all-reduce(f32[8,128]{1,0:T(8,128)S(1)} %get-tuple-element.13), channel_id=1, replica_groups=mesh['cache'=16,'proj'=16] {'cache'}, use_global_device_ids=true, to_apply=%region_6.7 | all-reduce | flops 1024 | bytes 8192 | tf_op jit(solution)/shard_map/pmax | solution.py:93
  229.7 3.4 fusion
  233.1 0.0 all-reduce.5.cloned.1.call-update
  233.1 0.0 reduce-scatter.2.cloned.1.call-start
  233.2 0.4 fusion.8
  233.6 28.6 %psum.23 = f32[8,128]{1,0:T(8,128)S(1)} all-reduce(f32[8,128]{1,0:T(8,128)S(1)} %fusion.8), channel_id=1, replica_groups=mesh['cache'=16,'proj'=16] {'cache'}, use_global_device_ids=true, to_apply=%region_9.10 | all-reduce | flops 1024 | bytes 8192 | tf_op jit(solution)/shard_map/psum | solution.py:102
  262.1 73.3 %all-reduce.5.cloned.1.call-done = f32[8,128,512]{2,1,0:T(8,128)} async-done(((f32[8,128,512]{2,1,0:T(8,128)}), f32[8,128,512]{2,1,0:T(8,128)}) %all-reduce.5.cloned.1.call-update) | async-done | bytes 2097168 | tf_op jit(solution)/shard_map/psum | solution.py:102
  335.4 1.8 divide_convert_fusion
  337.2 0.0 copy-start.2
  337.2 0.6 copy.65
  337.8 0.0 copy-start.3
  337.8 37.3 %all_to_all.54 = bf16[8,128,512]{2,0,1:T(8,128)(2,1)S(1)} all-to-all(bf16[8,128,512]{2,0,1:T(8,128)(2,1)S(1)} %copy.65), channel_id=1, replica_groups=mesh['cache'=16,'proj'=16] {'proj'}, dimensions={1} | all-to-all | bytes 2097152 | tf_op jit(solution)/shard_map/all_to_all | solution.py:104
  375.1 0.5 convolution_convert_fusion.1
  375.6 0.0 copy-done.3
  375.6 1.1 fusion.34
  376.7 0.0 reduce-scatter.2.cloned.1.call-update
  376.8 48.1 %reduce-scatter.2.cloned.1.call-done = f32[8,448]{1,0:T(8,128)} async-done(((f32[128,448]{1,0:T(8,128)}), f32[8,448]{1,0:T(8,128)}) %reduce-scatter.2.cloned.1.call-update) | async-done | bytes 14352 | tf_op jit(solution)/shard_map/reduce_scatter | solution.py:111
  424.8 1.3 convert_element_type.45
  (16 shorter events, 0.1 us)
Async XLA Ops:
  6.5 117.4 %copy-start = (bf16[8,128,512]{2,1,0:T(8,128)(2,1)S(1)}, bf16[8,128,512]{2,1,0:T(8,128)(2,1)}, u32[]{:S(2)}) copy-start(bf16[8,128,512]{2,1,0:T(8,128)(2,1)} %param.13) | copy-start | bytes 3145732
  6.5 105.5 %all-reduce.3.cloned.1.call-start = ((), (), s32[]{:S(2)}) async-start(), calls=%async_computation.4 | async-start | bytes 2097152 | tf_op jit(solution)/shard_map/psum | solution.py:60
  7.7 4.7 %copy-start.6 = (s32[128]{0:T(128)S(1)}, s32[128]{0:T(128)}, u32[]{:S(2)}) copy-start(s32[128]{0:T(128)} %param.17) | copy-start | bytes 1540
  112.0 12.0 %copy-start.1 = (f32[128,8,192]{2,0,1:T(8,128)S(1)}, f32[128,8,192]{2,0,1:T(8,128)}, u32[]{:S(2)}) copy-start(f32[128,8,192]{2,0,1:T(8,128)} %all-reduce.3.cloned.1.call-done) | copy-start | bytes 2359300
  114.8 18.4 %all-to-all-start.1 = ((bf16[16,2,2048]{2,1,0:T(2,128)(2,1)}), bf16[16,2,2048]{2,1,0:T(2,128)(2,1)S(1)}, u32[]{:S(2)}, u32[]{:S(2)}) async-start(bf16[16,2,2048]{2,1,0:T(2,128)(2,1)} %reshape.237), calls=%async_computation.1 | async-start | bytes 262144 | tf_op jit(solution)/shard_map/all_to_all | solution.py:64
  124.4 12.3 %copy-start.4 = (s32[8,32]{1,0:T(8,128)S(1)}, s32[8,32]{1,0:T(8,128)}, u32[]{:S(2)}) copy-start(s32[8,32]{1,0:T(8,128)} %param.18) | copy-start | bytes 3076
  124.4 12.3 %copy-start.5 = (s32[8]{0:T(128)S(1)}, s32[8]{0:T(128)}, u32[]{:S(2)}) copy-start(s32[8]{0:T(128)} %param.19) | copy-start | bytes 100
  133.1 61.1 %all-to-all-start = ((bf16[128,8,512]{2,1,0:T(8,128)(2,1)}), bf16[128,8,512]{2,1,0:T(8,128)(2,1)S(1)}, u32[]{:S(2)}, u32[]{:S(2)}) async-start(bf16[128,8,512]{2,1,0:T(8,128)(2,1)} %copy.57), calls=%async_computation | async-start | bytes 2097152 | tf_op jit(solution)/shard_map/all_to_all | solution.py:63
  136.7 198.7 %all-reduce.5.cloned.1.call-start = ((), (), s32[]{:S(2)}) async-start(), calls=%async_computation.5 | async-start | bytes 4194304 | tf_op jit(solution)/shard_map/psum | solution.py:102
  233.1 191.7 %reduce-scatter.2.cloned.1.call-start = ((), (), s32[]{:S(2)}) async-start(), calls=%async_computation.6 | async-start | bytes 278528 | tf_op jit(solution)/shard_map/reduce_scatter | solution.py:111
  337.2 37.9 %copy-start.2 = (bf16[8,512,128]{2,1,0:T(8,128)(2,1)S(1)}, bf16[8,512,128]{2,1,0:T(8,128)(2,1)}, u32[]{:S(2)}) copy-start(bf16[8,512,128]{2,1,0:T(8,128)(2,1)} %param.14) | copy-start | bytes 3145732
  337.8 37.8 %copy-start.3 = (bf16[1024,448]{0,1:T(8,128)(2,1)S(1)}, bf16[1024,448]{0,1:T(8,128)(2,1)}, u32[]{:S(2)}) copy-start(bf16[1024,448]{0,1:T(8,128)(2,1)} %param.15) | copy-start | bytes 2752516
Sparse Core Ops, SparseCore 0:
  12.5 99.4 all-reduce.2
  233.2 102.1 all-reduce.4
  376.9 47.9 reduce-scatter.1
where the time goes:
time: 436 us; the launch traced here: 433 us
  waiting for transfers between devices  228 us (52%)
  blocking collectives  96.8 us (22%)
  local copies, waits for them, and re-layouts  60.5 us (14%)
  between operations  13.4 us (3%)
  starting transfers between devices  12.8 us (3%)
  other arithmetic  11.5 us (3%)
  matrix products  9.91 us (2%)
    psum x1, waiting for transfers between devices, on_device(): query = lax.psum(partial_query, 'cache')  99.3 us
    psum x1, waiting for transfers between devices, on_device(): whole_total, whole_sum = lax.psum((total, summed), 'cache')  73.3 us
    reduce_scatter x1, waiting for transfers between devices, on_device(): lax.psum_scatter(jnp.dot(flat_values, w_output, preferred_element_type=jn...  48.1 us
    gather x1, local copies, waits for them, and re-layouts, on_device(): keys = jnp.take_along_axis(latent_cache, offsets[:, :, None], axis=1)  38.4 us
    all_to_all x1, blocking collectives, on_device(): lax.all_to_all(attended_latent_rows, 'proj', split_axis=1, concat_axis=0,...  37.3 us
    pmax x1, blocking collectives, on_device(): top = lax.pmax(largest, 'cache')  30.9 us
    psum x1, blocking collectives, on_device(): whole_total, whole_sum = lax.psum((total, summed), 'cache')  28.6 us
    unnamed x18, local copies, waits for them, and re-layouts  15.3 us
  transfers between devices with their start and end apart: 5, of which 4 were waited for; matrix products, arithmetic and copies ran while one was open for 14% of the time, Pallas kernels for 0%

commit v1 on v0

v1 whole, which is shorter than its diff:
```python
import functools

import jax
import jax.numpy as jnp
from jax import lax
from jax.experimental import pallas as pl
from jax.experimental.pallas import tpu as pltpu
from jax.sharding import PartitionSpec as P

NOPE = 128
ROPE = 64
KVR = 512
QK = KVR + ROPE
HEAD = NOPE + ROPE
BLK = 64
SLOTS = 4
ROWS = 8
HEADS = 8
LANES = 128
MESH = pl.DeviceIdType.MESH
F32 = jnp.float32
BF16 = jnp.bfloat16


def kernel(
    n,
    lens,
    ids,
    counts,
    cq_hbm,
    gain,
    wq_hbm,
    wk_hbm,
    vup_hbm,
    wo_hbm,
    cache_hbm,
    out,
    cq,
    wq,
    wk,
    vup,
    wo,
    cache,
    keys,
    tokens_at,
    a_send,
    a_recv,
    q_rows,
    b_send,
    q_all,
    o_send,
    l_send,
    o_recv,
    l_recv,
    f_send,
    f_recv,
    f_rows,
    v_all,
    h_send,
    h_recv,
    local_sem,
    a_ss,
    a_rs,
    b_sem,
    c_ss,
    c_rs,
    e_ss,
    e_rs,
    l_ss,
    l_rs,
    f_sem,
    g_ss,
    g_rs,
    h_ss,
    h_rs,
):
    c = lax.axis_index("cache")
    p = lax.axis_index("proj")
    barrier = pltpu.get_barrier_semaphore()

    def greet(i, carry):
        pl.semaphore_signal(
            barrier, inc=1, device_id=(lax.rem(c + i, n), p), device_id_type=MESH
        )
        pl.semaphore_signal(
            barrier, inc=1, device_id=(c, lax.rem(p + i, n)), device_id_type=MESH
        )
        return carry

    lax.fori_loop(1, n, greet, 0)

    depth = wq_hbm.shape[0]
    width = cq.shape[1]
    span = wq.shape[0]
    start = jnp.minimum((c * depth) // 128 * 128, width - span)
    inside = c * depth - start
    wq[...] = jnp.zeros_like(wq)
    loads = [
        pltpu.make_async_copy(cq_hbm, cq, local_sem.at[0]),
        pltpu.make_async_copy(
            wq_hbm, wq.at[pl.ds(pl.multiple_of(inside, 32), depth)], local_sem.at[1]
        ),
        pltpu.make_async_copy(wk_hbm, wk, local_sem.at[2]),
        pltpu.make_async_copy(cache_hbm, cache, local_sem.at[3]),
        pltpu.make_async_copy(vup_hbm, vup, local_sem.at[4]),
        pltpu.make_async_copy(wo_hbm, wo, local_sem.at[5]),
    ]
    for load in loads:
        load.start()

    loads[0].wait()
    source = cq[...].astype(F32)
    norm = lax.rsqrt(jnp.mean(source * source, -1, keepdims=True) + 1e-06)
    share = pl.ds(pl.multiple_of(start, 128), span)
    tiles = [gain[pl.ds(start // LANES + t, 1), :] for t in range(span // LANES)]
    normed = (cq[:, share].astype(F32) * norm * jnp.concatenate(tiles, 1)).astype(BF16)
    loads[1].wait()
    half = a_send.shape[2]
    tile = 256
    for t in range(half // tile):
        left = jnp.dot(normed, wq[:, t * tile : (t + 1) * tile], preferred_element_type=F32)
        right = jnp.dot(
            normed, wq[:, half + t * tile : half + (t + 1) * tile], preferred_element_type=F32
        )
        both = jnp.concatenate(
            [left.reshape(n, ROWS, tile), right.reshape(n, ROWS, tile)], axis=1
        )
        a_send[:, :, t * tile : (t + 1) * tile] = both.astype(BF16)

    pl.semaphore_wait(barrier, 2 * (n - 1))

    def a_copy(i):
        d = lax.rem(c + i, n)
        return pltpu.make_async_remote_copy(
            src_ref=a_send.at[lax.rem(d + p, n)],
            dst_ref=a_recv.at[c],
            send_sem=a_ss.at[i],
            recv_sem=a_rs.at[c],
            device_id=(d, p),
            device_id_type=MESH,
        )

    def start_all(make):
        def body(i, carry):
            make(i).start()
            return carry

        lax.fori_loop(1, n, body, 0)

    def finish_sends(make):
        def body(i, carry):
            make(i).wait_send()
            return carry

        lax.fori_loop(1, n, body, 0)

    def arrived(buffer, sems, s):
        pltpu.make_async_copy(buffer.at[s], buffer.at[s], sems.at[s]).wait()

    start_all(a_copy)

    ctx_local = cache.shape[2]
    per_shard = ctx_local // BLK
    slots = ids.shape[1]
    tokens = SLOTS * BLK

    def column(ref, base):
        rows = lax.broadcasted_iota(jnp.int32, (ROWS, 1), 0)
        found = jnp.zeros((ROWS, 1), jnp.int32)
        for r in range(ROWS):
            found = jnp.where(rows == r, ref[base + r], found)
        return found

    local = ids[...] - c * per_shard
    slot = lax.broadcasted_iota(jnp.int32, (ROWS, slots), 1)
    mine = (slot < column(counts, 0)) & (local >= 0) & (local < per_shard)
    before = lax.broadcasted_iota(jnp.int32, (slots, slots), 0) < lax.broadcasted_iota(
        jnp.int32, (slots, slots), 1
    )
    order = jnp.dot(
        mine.astype(F32), before.astype(F32), preferred_element_type=F32
    )
    lane = lax.broadcasted_iota(jnp.int32, (ROWS, tokens), 1)
    picked = jnp.full((ROWS, tokens), -1, jnp.int32)
    for k in range(SLOTS):
        kept = mine & (order == float(k))
        found = jnp.sum(jnp.where(kept, local + 1, 0), -1, keepdims=True) - 1
        picked = jnp.where(lane // BLK == k, found, picked)
    at = picked * BLK + lane % BLK
    live_at = (picked >= 0) & (c * ctx_local + at < column(lens, p * ROWS))
    tokens_at[...] = jnp.where(live_at, at, -1)

    loads[3].wait()

    def gather(r, carry):
        chosen = lax.broadcasted_iota(jnp.int32, (ctx_local, tokens), 0) == tokens_at[
            pl.ds(r, 1), :
        ]
        keys[r] = jnp.dot(
            cache[r], chosen.astype(F32).astype(BF16), preferred_element_type=F32
        ).astype(BF16)
        return carry

    lax.fori_loop(0, ROWS, gather, 0)

    block = lax.rem(c + p, n)

    def add(i, total):
        s = lax.rem(c + i, n)
        arrived(a_recv, a_rs, s)
        return total + a_recv[s].astype(F32)

    query = lax.fori_loop(1, n, add, a_send[block].astype(F32))
    half_rope = ROPE // 2
    index = lax.broadcasted_iota(jnp.int32, (1, half_rope), 1)
    freq = jnp.zeros((1, half_rope), F32)
    for i in range(half_rope):
        freq = jnp.where(index == i, float(10000.0 ** (-2.0 * i / ROPE)), freq)
    angles = (column(lens, block * ROWS) - 1).astype(F32) * freq
    angles = jnp.concatenate([angles, angles], axis=0)
    cosine, sine = jnp.cos(angles), jnp.sin(angles)
    loads[2].wait()
    per_half = HEADS // 2
    blank = jnp.zeros((2 * ROWS, LANES - ROPE), F32)
    for j in range(per_half):
        base = j * HEAD
        nope = query[:, base : base + NOPE].astype(BF16)
        first = query[:, base + NOPE : base + NOPE + ROPE // 2]
        second = query[:, base + NOPE + ROPE // 2 : base + HEAD]
        turned = jnp.concatenate(
            [first * cosine - second * sine, first * sine + second * cosine, blank], axis=1
        )
        for g in range(2):
            h = g * per_half + j
            latent = jnp.dot(nope, wk[h], preferred_element_type=F32)
            place = pl.ds(h, ROWS, stride=HEADS)
            for t in range(KVR // LANES):
                q_rows[t, place, :] = latent[g * ROWS : (g + 1) * ROWS, t * LANES : (t + 1) * LANES]
            q_rows[KVR // LANES, place, :] = turned[g * ROWS : (g + 1) * ROWS]
    for t in range(KVR // LANES):
        b_send[:, t * LANES : (t + 1) * LANES] = q_rows[t].astype(BF16)
    b_send[:, KVR:] = q_rows[KVR // LANES][:, :ROPE].astype(BF16)

    def b_remote():
        return pltpu.make_async_remote_copy(
            src_ref=b_send,
            dst_ref=q_all.at[c],
            send_sem=b_sem.at[0],
            recv_sem=b_sem.at[1],
            device_id=(c, block),
            device_id_type=MESH,
        )

    @pl.when(c != 0)
    def _():
        copy = b_remote()
        copy.start()
        copy.wait_recv()

    @pl.when(c == 0)
    def _():
        q_all[c] = b_send[...]

    def c_copy(i):
        d = lax.rem(c + i, n)
        return pltpu.make_async_remote_copy(
            src_ref=q_all.at[c],
            dst_ref=q_all.at[c],
            send_sem=c_ss.at[i],
            recv_sem=c_rs.at[c],
            device_id=(d, p),
            device_id_type=MESH,
        )

    start_all(c_copy)

    def c_wait(i, carry):
        arrived(q_all, c_rs, lax.rem(c + i, n))
        return carry

    lax.fori_loop(1, n, c_wait, 0)

    scale = HEAD ** (-0.5)
    heads = n * HEADS
    eye = lax.broadcasted_iota(jnp.int32, (heads, heads), 0) == lax.broadcasted_iota(
        jnp.int32, (heads, heads), 1
    )

    def attend(r, q):
        live = tokens_at[pl.ds(r, 1), :] >= 0
        key = keys[r]
        scores = jnp.dot(q, key, preferred_element_type=F32) * scale
        largest = jnp.max(jnp.where(live, scores, -1e30), -1, keepdims=True)
        weights = jnp.where(live, jnp.exp(scores - largest), 0.0)
        total = jnp.sum(weights, -1, keepdims=True)
        summed = lax.dot_general(
            weights.astype(BF16),
            key[:KVR],
            (((1,), (1,)), ((), ())),
            preferred_element_type=F32,
        )
        some = total > 0.0
        safe = jnp.where(some, total, 1.0)
        logs = jnp.where(some, largest + jnp.log(safe), -1e30)
        l_send[pl.ds(r, 1), :] = jnp.sum(jnp.where(eye, logs, 0.0), 0, keepdims=True)
        return summed * (1.0 / safe)

    def pair(m, carry):
        two = pl.ds(pl.multiple_of(m * 16, 16), 16)
        q = q_all[:, two, :].astype(F32)
        first = attend(2 * m, q[:, :ROWS, :].reshape(heads, QK).astype(BF16))
        second = attend(2 * m + 1, q[:, ROWS:, :].reshape(heads, QK).astype(BF16))
        o_send[:, two, :] = jnp.concatenate(
            [first.reshape(n, HEADS, KVR), second.reshape(n, HEADS, KVR)], axis=1
        ).astype(BF16)
        return carry

    lax.fori_loop(0, ROWS // 2, pair, 0)

    def e_copy(i):
        d = lax.rem(c + i, n)
        return pltpu.make_async_remote_copy(
            src_ref=o_send.at[d],
            dst_ref=o_recv.at[c],
            send_sem=e_ss.at[i],
            recv_sem=e_rs.at[c],
            device_id=(d, p),
            device_id_type=MESH,
        )

    def l_copy(i):
        d = lax.rem(c + i, n)
        return pltpu.make_async_remote_copy(
            src_ref=l_send,
            dst_ref=l_recv.at[c],
            send_sem=l_ss.at[i],
            recv_sem=l_rs.at[c],
            device_id=(d, p),
            device_id_type=MESH,
        )

    start_all(l_copy)
    start_all(e_copy)
    o_recv[c] = o_send[c]
    l_recv[c] = l_send[...]

    def l_wait(i, carry):
        arrived(l_recv, l_rs, lax.rem(c + i, n))
        return carry

    lax.fori_loop(1, n, l_wait, 0)
    logs = l_recv[...]
    raised = jnp.exp(logs - jnp.max(logs, 0, keepdims=True))
    l_recv[...] = raised / jnp.sum(raised, 0, keepdims=True)
    own = ROWS * HEADS
    mask = (
        lax.broadcasted_iota(jnp.int32, (own, heads), 1)
        == c * HEADS + lax.broadcasted_iota(jnp.int32, (own, heads), 0) % HEADS
    )

    def weigh(s):
        factor = jnp.broadcast_to(l_recv[s][:, None, :], (ROWS, HEADS, heads)).reshape(own, heads)
        column = jnp.sum(jnp.where(mask, factor, 0.0), -1, keepdims=True)
        return o_recv[s].astype(F32) * column

    def combine(i, total):
        s = lax.rem(c + i, n)
        arrived(o_recv, e_rs, s)
        return total + weigh(s)

    attended = lax.fori_loop(1, n, combine, weigh(c))
    f_send[...] = attended.astype(BF16)

    def f_remote():
        return pltpu.make_async_remote_copy(
            src_ref=f_send,
            dst_ref=f_recv,
            send_sem=f_sem.at[0],
            recv_sem=f_sem.at[1],
            device_id=(c, lax.rem(p + n - c, n)),
            device_id_type=MESH,
        )

    @pl.when(c != 0)
    def _():
        copy = f_remote()
        copy.start()
        copy.wait_recv()

    @pl.when(c == 0)
    def _():
        f_recv[...] = f_send[...]

    loads[4].wait()
    for t in range(KVR // LANES):
        f_rows[t] = f_recv[:, t * LANES : (t + 1) * LANES].astype(F32)
    values = [
        jnp.dot(
            jnp.concatenate(
                [f_rows[t, pl.ds(h, ROWS, stride=HEADS), :] for t in range(KVR // LANES)], 1
            ).astype(BF16),
            vup[h],
            preferred_element_type=F32,
        )
        for h in range(HEADS)
    ]
    v_all[c] = jnp.concatenate(
        [jnp.concatenate(values[:per_half], 1), jnp.concatenate(values[per_half:], 1)], 0
    ).astype(BF16)

    def g_copy(i):
        d = lax.rem(c + i, n)
        return pltpu.make_async_remote_copy(
            src_ref=v_all.at[c],
            dst_ref=v_all.at[c],
            send_sem=g_ss.at[i],
            recv_sem=g_rs.at[c],
            device_id=(d, p),
            device_id_type=MESH,
        )

    start_all(g_copy)
    loads[5].wait()

    def g_wait(i, carry):
        arrived(v_all, g_rs, lax.rem(c + i, n))
        return carry

    lax.fori_loop(1, n, g_wait, 0)

    v = v_all[...].astype(F32)
    wide = v.shape[2]
    rows = n * ROWS
    low = v[:, :ROWS, :].reshape(rows, wide).astype(BF16)
    high = v[:, ROWS:, :].reshape(rows, wide).astype(BF16)
    across = (((1,), (1,)), ((), ()))
    result = lax.dot_general(
        low, wo[:, :wide], across, preferred_element_type=F32
    ) + lax.dot_general(high, wo[:, wide:], across, preferred_element_type=F32)
    columns = wo.shape[0]
    cut = h_send.shape[2]
    rest = jnp.concatenate(
        [result[:, cut:], jnp.zeros((rows, 2 * cut - columns), F32)], axis=1
    )
    h_send[...] = jnp.concatenate(
        [result[:, :cut].reshape(n, ROWS, cut), rest.reshape(n, ROWS, cut)], axis=1
    ).astype(BF16)

    def h_copy(i):
        return pltpu.make_async_remote_copy(
            src_ref=h_send.at[i],
            dst_ref=h_recv.at[p],
            send_sem=h_ss.at[i],
            recv_sem=h_rs.at[p],
            device_id=(c, lax.rem(p + i, n)),
            device_id_type=MESH,
        )

    start_all(h_copy)

    def h_add(i, total):
        s = lax.rem(p + i, n)
        arrived(h_recv, h_rs, s)
        return total + h_recv[s].astype(F32)

    summed = lax.fori_loop(1, n, h_add, h_send[0].astype(F32))
    out[...] = jnp.concatenate(
        [summed[:ROWS], summed[ROWS:, : columns - cut]], axis=1
    ).astype(BF16)

    for make in (a_copy, c_copy, e_copy, l_copy, g_copy, h_copy):
        finish_sends(make)

    @pl.when(c != 0)
    def _():
        b_remote().wait_send()
        f_remote().wait_send()


def on_device(
    compressed_query,
    query_gain,
    w_query,
    w_key,
    value_up_weight,
    w_output,
    latent_cache,
    context_lengths,
    block_ids,
    block_counts,
):
    n = lax.axis_size("cache")
    rows, rank = compressed_query.shape
    depth, columns = w_query.shape
    span = 256
    w_output = w_output.T
    latent_cache = latent_cache.transpose(0, 2, 1)
    heads = n * HEADS
    own = ROWS * HEADS
    out_columns = w_output.shape[0]
    smem = pl.BlockSpec(memory_space=pltpu.SMEM)
    vmem = pl.BlockSpec(memory_space=pltpu.VMEM)
    hbm = pl.BlockSpec(memory_space=pl.ANY)
    many = pltpu.SemaphoreType.DMA((n,))
    two = pltpu.SemaphoreType.DMA((2,))
    return pl.pallas_call(
        functools.partial(kernel, n),
        out_shape=jax.ShapeDtypeStruct((ROWS, out_columns), BF16),
        in_specs=[smem, vmem, smem, hbm, vmem, hbm, hbm, hbm, hbm, hbm],
        out_specs=vmem,
        scratch_shapes=[
            pltpu.VMEM((rows, rank), BF16),
            pltpu.VMEM((span, columns), BF16),
            pltpu.VMEM(w_key.shape, BF16),
            pltpu.VMEM(value_up_weight.shape, BF16),
            pltpu.VMEM(w_output.shape, BF16),
            pltpu.VMEM(latent_cache.shape, BF16),
            pltpu.VMEM((ROWS, QK, SLOTS * BLK), BF16),
            pltpu.VMEM((ROWS, SLOTS * BLK), jnp.int32),
            pltpu.VMEM((n, 2 * ROWS, columns // 2), BF16),
            pltpu.VMEM((n, 2 * ROWS, columns // 2), BF16),
            pltpu.VMEM((KVR // LANES + 1, own, LANES), F32),
            pltpu.VMEM((own, QK), BF16),
            pltpu.VMEM((n, own, QK), BF16),
            pltpu.VMEM((n, own, KVR), BF16),
            pltpu.VMEM((ROWS, heads), F32),
            pltpu.VMEM((n, own, KVR), BF16),
            pltpu.VMEM((n, ROWS, heads), F32),
            pltpu.VMEM((own, KVR), BF16),
            pltpu.VMEM((own, KVR), BF16),
            pltpu.VMEM((KVR // LANES, own, LANES), F32),
            pltpu.VMEM((n, 2 * ROWS, HEADS // 2 * NOPE), BF16),
            pltpu.VMEM((n, 2 * ROWS, 256), BF16),
            pltpu.VMEM((n, 2 * ROWS, 256), BF16),
            pltpu.SemaphoreType.DMA((6,)),
            many,
            many,
            two,
            many,
            many,
            many,
            many,
            many,
            many,
            two,
            many,
            many,
            many,
            many,
        ],
        compiler_params=pltpu.CompilerParams(
            collective_id=0, has_side_effects=True, vmem_limit_bytes=56 * 2**20
        ),
    )(
        context_lengths,
        block_ids,
        block_counts,
        compressed_query,
        query_gain.reshape(rank // LANES, LANES),
        w_query,
        w_key,
        value_up_weight,
        w_output,
        latent_cache,
    )


def solution(mesh):
    placed = (
        P(),
        P(),
        P("cache", "proj"),
        P("proj", None, None),
        P("proj", None, None),
        P("proj", "cache"),
        P("proj", "cache", None),
        P(),
        P("proj", None),
        P("proj"),
    )
    return jax.shard_map(
        on_device, mesh=mesh, in_specs=placed, out_specs=P("proj", "cache"), check_vma=False
    )
```

time: 436 us -> 83.5 us (0.19)
  waiting for transfers between devices: 228 us -> 0 us
  blocking collectives: 96.8 us -> 0 us
  Pallas kernels: 0 us -> 82 us
  local copies, waits for them, and re-layouts: 60.5 us -> 1.3 us
  between operations: 13.4 us -> 0.01 us
  starting transfers between devices: 12.8 us -> 0 us
  other arithmetic: 11.5 us -> 0 us
  matrix products: 9.91 us -> 0 us
    psum x2 -> x0, waiting for transfers between devices: 173 us -> none  [the longest x1 99.3 us: on_device(): query = lax.psum(partial_query, 'cache')]
    pallas_call x0 -> x1, Pallas kernels: none -> 82 us  [on_device(): pl.pallas_call(functools.partial(kernel, n), out_shape=jax.ShapeDtypeStru...]
    reduce_scatter x1 -> x0, waiting for transfers between devices: 48.1 us -> none  [on_device(): lax.psum_scatter(jnp.dot(flat_values, w_output, preferred_element_type=jn...]
    gather x1 -> x0, local copies, waits for them, and re-layouts: 38.4 us -> none  [on_device(): keys = jnp.take_along_axis(latent_cache, offsets[:, :, None], axis=1)]
    all_to_all x1 -> x0, blocking collectives: 37.3 us -> none  [on_device(): lax.all_to_all(attended_latent_rows, 'proj', split_axis=1, concat_axis=0,...]
    pmax x1 -> x0, blocking collectives: 30.9 us -> none  [on_device(): top = lax.pmax(largest, 'cache')]
    psum x1 -> x0, blocking collectives: 28.6 us -> none  [on_device(): whole_total, whole_sum = lax.psum((total, summed), 'cache')]
    unnamed x18 -> x1, local copies, waits for them, and re-layouts: 15.3 us -> 1.3 us
  transfers between devices with their start and end apart: 5 -> 0, of which waited for: 4 -> 0; matrix products, arithmetic and copies ran while one was open for 14% -> 0% of each run, Pallas kernels for 0% -> 0%
where the time goes in v1:
time: 83.5 us; the launch traced here: 83.3 us
  Pallas kernels  82 us (98%)
  local copies, waits for them, and re-layouts  1.3 us (2%)
    pallas_call x1, Pallas kernels, on_device(): pl.pallas_call(functools.partial(kernel, n), out_shape=jax.ShapeDtypeStru...  82 us

profile of v1, /device:TPU:1, one launch (start us, length us, event | category | flops | bytes accessed | tf_op | source)
XLA Modules:
  0.0 83.3 jit_solution(2712533615602883484)
XLA Ops:
  0.0 82.0 %shard_map.100 = bf16[8,448]{1,0:T(8,128)(2,1)} custom-call(s32[128]{0:T(128)} %lens.1, s32[8,32]{1,0:T(8,128)} %ids.1, s32[8]{0:T(128)} %counts.1, bf16[128,1536]{1,0:T(8,128)(2,1)} %cq_hbm.1, f32[12,128]{1,0:T(8,128)} %bitcast.5, bf16[96,1536]{1,0:T(8,128)(2,1)} %wq_hbm.1, bf16[8,128,512]{2,1,0:T(8,128)(2,1)} %wk_hbm.1, bf16[8,512,128]{2,1,0:T(8,128)(2,1)} %vup_hbm.1, ...), custom_call_target="tpu_custom_call" | custom-call | tf_op jit(solution)/shard_map/pallas_call | solution.py:506
  82.0 1.3 %copy.12 = bf16[8,448]{1,0:T(8,128)(2,1)} copy(bf16[8,448]{1,0:T(8,128)(2,1)} %shard_map.100) | data formatting | bytes 14336

commit v2 on v1

--- a/solution.py
+++ b/solution.py
@@ -17,6 +17,12 @@
 ROWS = 8
 HEADS = 8
 LANES = 128
+SIDE = 4
+RING = (1, 3, 2)
+FAR_FIRST = sorted(
+    [(i, j) for i in range(SIDE) for j in range(SIDE) if i or j],
+    key=lambda at: -min(at[0], SIDE - at[0]) - min(at[1], SIDE - at[1]),
+)
 MESH = pl.DeviceIdType.MESH
 F32 = jnp.float32
 BF16 = jnp.bfloat16
@@ -49,9 +55,14 @@
     b_send,
     q_all,
     o_send,
+    o_first,
+    o_merged,
+    o_second,
     l_send,
-    o_recv,
-    l_recv,
+    l_first,
+    l_ratio,
+    l_next,
+    l_second,
     f_send,
     f_recv,
     f_rows,
@@ -61,11 +72,14 @@
     local_sem,
     a_ss,
     a_rs,
-    b_sem,
+    b_ss,
+    b_rs,
     c_ss,
     c_rs,
     e_ss,
     e_rs,
+    e2_ss,
+    e2_rs,
     l_ss,
     l_rs,
     f_sem,
@@ -76,6 +90,38 @@
 ):
     c = lax.axis_index("cache")
     p = lax.axis_index("proj")
+    x, y = c // SIDE, lax.rem(c, SIDE)
+
+    def on_x(i):
+        return lax.rem(x + i, SIDE) * SIDE + y
+
+    def on_y(i):
+        return x * SIDE + lax.rem(y + i, SIDE)
+
+    def on_plane(k):
+        dx, dy = FAR_FIRST[k]
+        return lax.rem(x + dx, SIDE) * SIDE + lax.rem(y + dy, SIDE)
+
+    def send(src, dst, send_sem, recv_sem, cache_at, proj_at):
+        return pltpu.make_async_remote_copy(
+            src_ref=src,
+            dst_ref=dst,
+            send_sem=send_sem,
+            recv_sem=recv_sem,
+            device_id=(cache_at, proj_at),
+            device_id_type=MESH,
+        )
+
+    def arrived(ref, sem):
+        pltpu.make_async_copy(ref, ref, sem).wait()
+
+    sent = []
+
+    def go(*copy):
+        copy = send(*copy)
+        copy.start()
+        sent.append(copy)
+
     barrier = pltpu.get_barrier_semaphore()
 
     def greet(i, carry):
@@ -129,35 +175,9 @@
 
     pl.semaphore_wait(barrier, 2 * (n - 1))
 
-    def a_copy(i):
-        d = lax.rem(c + i, n)
-        return pltpu.make_async_remote_copy(
-            src_ref=a_send.at[lax.rem(d + p, n)],
-            dst_ref=a_recv.at[c],
-            send_sem=a_ss.at[i],
-            recv_sem=a_rs.at[c],
-            device_id=(d, p),
-            device_id_type=MESH,
-        )
-
-    def start_all(make):
-        def body(i, carry):
-            make(i).start()
-            return carry
-
-        lax.fori_loop(1, n, body, 0)
-
-    def finish_sends(make):
-        def body(i, carry):
-            make(i).wait_send()
-            return carry
-
-        lax.fori_loop(1, n, body, 0)
-
-    def arrived(buffer, sems, s):
-        pltpu.make_async_copy(buffer.at[s], buffer.at[s], sems.at[s]).wait()
-
-    start_all(a_copy)
+    for k in range(n - 1):
+        d = on_plane(k)
+        go(a_send.at[lax.rem(d + p, n)], a_recv.at[c], a_ss.at[k], a_rs.at[c], d, p)
 
     ctx_local = cache.shape[2]
     per_shard = ctx_local // BLK
@@ -207,7 +227,7 @@
 
     def add(i, total):
         s = lax.rem(c + i, n)
-        arrived(a_recv, a_rs, s)
+        arrived(a_recv.at[s], a_rs.at[s])
         return total + a_recv[s].astype(F32)
 
     query = lax.fori_loop(1, n, add, a_send[block].astype(F32))
@@ -237,48 +257,74 @@
             for t in range(KVR // LANES):
                 q_rows[t, place, :] = latent[g * ROWS : (g + 1) * ROWS, t * LANES : (t + 1) * LANES]
             q_rows[KVR // LANES, place, :] = turned[g * ROWS : (g + 1) * ROWS]
-    for t in range(KVR // LANES):
-        b_send[:, t * LANES : (t + 1) * LANES] = q_rows[t].astype(BF16)
-    b_send[:, KVR:] = q_rows[KVR // LANES][:, :ROPE].astype(BF16)
-
-    def b_remote():
-        return pltpu.make_async_remote_copy(
-            src_ref=b_send,
-            dst_ref=q_all.at[c],
-            send_sem=b_sem.at[0],
-            recv_sem=b_sem.at[1],
-            device_id=(c, block),
-            device_id_type=MESH,
-        )
+    own = ROWS * HEADS
+    part = own // 2
+    latent_tiles = KVR // LANES
+    for g in range(2):
+        for t in range(latent_tiles):
+            b_send[g, t * part : (t + 1) * part, :] = q_rows[
+                t, g * part : (g + 1) * part, :
+            ].astype(BF16)
+        low = q_rows[latent_tiles, g * part : g * part + part // 2, :]
+        high = q_rows[latent_tiles, g * part + part // 2 : (g + 1) * part, :]
+        b_send[g, latent_tiles * part :, :] = jnp.concatenate(
+            [low[:, :ROPE], high[:, :ROPE]], axis=1
+        ).astype(BF16)
+
+    def b_copy(g):
+        return send(b_send.at[g], q_all.at[c, g], b_ss.at[g], b_rs.at[g], c, block)
 
     @pl.when(c != 0)
     def _():
-        copy = b_remote()
-        copy.start()
-        copy.wait_recv()
+        b_copy(0).start()
+        b_copy(1).start()
 
     @pl.when(c == 0)
     def _():
         q_all[c] = b_send[...]
 
-    def c_copy(i):
-        d = lax.rem(c + i, n)
-        return pltpu.make_async_remote_copy(
-            src_ref=q_all.at[c],
-            dst_ref=q_all.at[c],
-            send_sem=c_ss.at[i],
-            recv_sem=c_rs.at[c],
-            device_id=(d, p),
-            device_id_type=MESH,
-        )
-
-    start_all(c_copy)
-
-    def c_wait(i, carry):
-        arrived(q_all, c_rs, lax.rem(c + i, n))
-        return carry
-
-    lax.fori_loop(1, n, c_wait, 0)
+    count = iter(range(30))
+
+    def spread(s, g, to):
+        k = next(count)
+        go(q_all.at[s, g], q_all.at[s, g], c_ss.at[k], c_rs.at[s, g], to, p)
+
+    def got(s, g):
+        arrived(q_all.at[s, g], c_rs.at[s, g])
+
+    @pl.when(c != 0)
+    def _():
+        b_copy(0).wait_recv()
+
+    for i in RING:
+        spread(c, 0, on_x(i))
+
+    @pl.when(c != 0)
+    def _():
+        b_copy(1).wait_recv()
+
+    for i in RING:
+        spread(c, 1, on_y(i))
+    for i in RING:
+        spread(c, 0, on_y(i))
+        spread(c, 1, on_x(i))
+    for i in RING:
+        s = on_x(i)
+        got(s, 0)
+        for j in RING:
+            spread(s, 0, on_y(j))
+        s = on_y(i)
+        got(s, 1)
+        for j in RING:
+            spread(s, 1, on_x(j))
+    for i in RING:
+        got(on_y(i), 0)
+        got(on_x(i), 1)
+    for dx, dy in FAR_FIRST:
+        if dx and dy:
+            s = lax.rem(x + dx, SIDE) * SIDE + lax.rem(y + dy, SIDE)
+            got(s, 0)
+            got(s, 1)
 
     scale = HEAD ** (-0.5)
     heads = n * HEADS
@@ -286,8 +332,10 @@
         jnp.int32, (heads, heads), 1
     )
 
+    half_count = ROWS // 2
+
     def attend(r, q):
-        live = tokens_at[pl.ds(r, 1), :] >= 0
+        live = tokens_at[r : r + 1, :] >= 0
         key = keys[r]
         scores = jnp.dot(q, key, preferred_element_type=F32) * scale
         largest = jnp.max(jnp.where(live, scores, -1e30), -1, keepdims=True)
@@ -302,90 +350,148 @@
         some = total > 0.0
         safe = jnp.where(some, total, 1.0)
         logs = jnp.where(some, largest + jnp.log(safe), -1e30)
-        l_send[pl.ds(r, 1), :] = jnp.sum(jnp.where(eye, logs, 0.0), 0, keepdims=True)
+        l_send[r // half_count, r % half_count : r % half_count + 1, :] = jnp.sum(jnp.where(eye, logs, 0.0), 0, keepdims=True)
         return summed * (1.0 / safe)
 
-    def pair(m, carry):
-        two = pl.ds(pl.multiple_of(m * 16, 16), 16)
-        q = q_all[:, two, :].astype(F32)
+    def pair(m):
+        g, j = m // 2, m % 2
+        tiles = [
+            q_all[:, g, t * part + j * 16 : t * part + j * 16 + 16, :] for t in range(latent_tiles)
+        ]
+        tiles.append(q_all[:, g, latent_tiles * part :, j * ROPE : (j + 1) * ROPE])
+        q = jnp.concatenate([tile.astype(F32) for tile in tiles], axis=2)
         first = attend(2 * m, q[:, :ROWS, :].reshape(heads, QK).astype(BF16))
         second = attend(2 * m + 1, q[:, ROWS:, :].reshape(heads, QK).astype(BF16))
-        o_send[:, two, :] = jnp.concatenate(
+        both = jnp.concatenate(
             [first.reshape(n, HEADS, KVR), second.reshape(n, HEADS, KVR)], axis=1
         ).astype(BF16)
-        return carry
-
-    lax.fori_loop(0, ROWS // 2, pair, 0)
-
-    def e_copy(i):
-        d = lax.rem(c + i, n)
-        return pltpu.make_async_remote_copy(
-            src_ref=o_send.at[d],
-            dst_ref=o_recv.at[c],
-            send_sem=e_ss.at[i],
-            recv_sem=e_rs.at[c],
-            device_id=(d, p),
-            device_id_type=MESH,
-        )
-
-    def l_copy(i):
-        d = lax.rem(c + i, n)
-        return pltpu.make_async_remote_copy(
-            src_ref=l_send,
-            dst_ref=l_recv.at[c],
-            send_sem=l_ss.at[i],
-            recv_sem=l_rs.at[c],
-            device_id=(d, p),
-            device_id_type=MESH,
-        )
-
-    start_all(l_copy)
-    start_all(e_copy)
-    o_recv[c] = o_send[c]
-    l_recv[c] = l_send[...]
-
-    def l_wait(i, carry):
-        arrived(l_recv, l_rs, lax.rem(c + i, n))
-        return carry
-
-    lax.fori_loop(1, n, l_wait, 0)
-    logs = l_recv[...]
-    raised = jnp.exp(logs - jnp.max(logs, 0, keepdims=True))
-    l_recv[...] = raised / jnp.sum(raised, 0, keepdims=True)
-    own = ROWS * HEADS
-    mask = (
-        lax.broadcasted_iota(jnp.int32, (own, heads), 1)
-        == c * HEADS + lax.broadcasted_iota(jnp.int32, (own, heads), 0) % HEADS
-    )
-
-    def weigh(s):
-        factor = jnp.broadcast_to(l_recv[s][:, None, :], (ROWS, HEADS, heads)).reshape(own, heads)
-        column = jnp.sum(jnp.where(mask, factor, 0.0), -1, keepdims=True)
-        return o_recv[s].astype(F32) * column
-
-    def combine(i, total):
-        s = lax.rem(c + i, n)
-        arrived(o_recv, e_rs, s)
-        return total + weigh(s)
-
-    attended = lax.fori_loop(1, n, combine, weigh(c))
-    f_send[...] = attended.astype(BF16)
-
-    def f_remote():
-        return pltpu.make_async_remote_copy(
-            src_ref=f_send,
-            dst_ref=f_recv,
-            send_sem=f_sem.at[0],
-            recv_sem=f_sem.at[1],
-            device_id=(c, lax.rem(p + n - c, n)),
-            device_id_type=MESH,
-        )
+        o_send[:, :, m * 16 : (m + 1) * 16, :] = both.reshape(SIDE, SIDE, 16, KVR)
+
+    def rows_of(g):
+        return pl.ds(g * part, part)
+
+    def piece(g, first, second):
+        here = (first, second) if g == 0 else (second, first)
+        return o_send.at[here[0], here[1], rows_of(g), :]
+
+    mine = (x, y)
+    along = (on_x, on_y)
+    count_1 = iter(range(24))
+    count_l = iter(range(12))
+
+    def first_stage(g):
+        for i in RING:
+            k = next(count_l)
+            go(l_send.at[g], l_first.at[g, mine[g]], l_ss.at[k], l_rs.at[g, 0, mine[g]], along[g](i), p)
+        for j in RING + (0,):
+            to = lax.rem(mine[1 - g] + j, SIDE)
+            for i in RING:
+                k = next(count_1)
+                at = lax.rem(mine[g] + i, SIDE)
+                go(
+                    piece(g, at, to),
+                    o_first.at[g, mine[g], to],
+                    e_ss.at[k],
+                    e_rs.at[g, mine[g], to],
+                    along[g](i),
+                    p,
+                )
+
+    for m in range(2):
+        pair(m)
+    first_stage(0)
+    for m in range(2, 4):
+        pair(m)
+    first_stage(1)
+
+    def shares(logs):
+        top = jnp.max(logs, 0, keepdims=True)
+        raised = jnp.exp(logs - top)
+        total = jnp.sum(raised, 0, keepdims=True)
+        return raised / total, (top + jnp.log(total))[0]
+
+    spot = lax.broadcasted_iota(jnp.int32, (part, heads), 1) - (
+        lax.broadcasted_iota(jnp.int32, (part, heads), 0) % HEADS
+    )
+
+    def scaled(value, share, d):
+        wide = jnp.broadcast_to(share[:, None, :], (half_count, HEADS, heads))
+        wide = wide.reshape(part, heads)
+        column = jnp.sum(jnp.where(spot == d * HEADS, wide, 0.0), -1, keepdims=True)
+        return value.astype(F32) * column
+
+    def slot_of(v, i):
+        return lax.rem(v + i, SIDE)
+
+    count_2 = iter(range(6))
+
+    def weights_of(buffer, g, stage, me):
+        for i in RING:
+            s = slot_of(me, i)
+            arrived(buffer.at[g, s], l_rs.at[g, stage, s])
+        return shares(buffer[g])
+
+    for g in range(2):
+        l_first[g, mine[g]] = l_send[g]
+    for g in range(2):
+        share, merged = weights_of(l_first, g, 0, mine[g])
+        l_ratio[g] = share
+        l_next[g] = merged
+        for i in RING:
+            k = next(count_l)
+            go(
+                l_next.at[g],
+                l_second.at[g, mine[1 - g]],
+                l_ss.at[k],
+                l_rs.at[g, 1, mine[1 - g]],
+                along[1 - g](i),
+                p,
+            )
+        l_second[g, mine[1 - g]] = merged
+
+    def merge(g, to):
+        at = (mine[0], to) if g == 0 else (to, mine[1])
+        d = at[0] * SIDE + at[1]
+        total = scaled(
+            o_send[at[0], at[1], g * part : (g + 1) * part, :], l_ratio[g, mine[g]], d
+        )
+        for i in RING:
+            s = slot_of(mine[g], i)
+            arrived(o_first.at[g, s, to], e_rs.at[g, s, to])
+            total = total + scaled(o_first[g, s, to], l_ratio[g, s], d)
+        return total
+
+    for j in RING:
+        for g in range(2):
+            to = slot_of(mine[1 - g], j)
+            o_merged[g, to] = merge(g, to).astype(BF16)
+            k = next(count_2)
+            go(
+                o_merged.at[g, to],
+                o_second.at[g, mine[1 - g]],
+                e2_ss.at[k],
+                e2_rs.at[g, mine[1 - g]],
+                along[1 - g](j),
+                p,
+            )
+    kept = [merge(g, mine[1 - g]) for g in range(2)]
+    for g in range(2):
+        share, _ = weights_of(l_second, g, 1, mine[1 - g])
+        l_ratio[g] = share
+        total = scaled(kept[g], l_ratio[g, mine[1 - g]], c)
+        for i in RING:
+            s = slot_of(mine[1 - g], i)
+            arrived(o_second.at[g, s], e2_rs.at[g, s])
+            total = total + scaled(o_second[g, s], l_ratio[g, s], c)
+        f_send[g * part : (g + 1) * part, :] = total.astype(BF16)
+
+    def f_copy():
+        return send(f_send, f_recv, f_sem.at[0], f_sem.at[1], c, lax.rem(p + n - c, n))
 
     @pl.when(c != 0)
     def _():
-        copy = f_remote()
-        copy.start()
-        copy.wait_recv()
+        f_copy().start()
+        f_copy().wait_recv()
 
     @pl.when(c == 0)
     def _():
@@ -408,25 +514,12 @@
         [jnp.concatenate(values[:per_half], 1), jnp.concatenate(values[per_half:], 1)], 0
     ).astype(BF16)
 
-    def g_copy(i):
-        d = lax.rem(c + i, n)
-        return pltpu.make_async_remote_copy(
-            src_ref=v_all.at[c],
-            dst_ref=v_all.at[c],
-            send_sem=g_ss.at[i],
-            recv_sem=g_rs.at[c],
-            device_id=(d, p),
-            device_id_type=MESH,
-        )
-
-    start_all(g_copy)
+    for k in range(n - 1):
+        go(v_all.at[c], v_all.at[c], g_ss.at[k], g_rs.at[c], on_plane(k), p)
     loads[5].wait()
-
-    def g_wait(i, carry):
-        arrived(v_all, g_rs, lax.rem(c + i, n))
-        return carry
-
-    lax.fori_loop(1, n, g_wait, 0)
+    for k in reversed(range(n - 1)):
+        d = on_plane(k)
+        arrived(v_all.at[d], g_rs.at[d])
 
     v = v_all[...].astype(F32)
     wide = v.shape[2]
@@ -446,21 +539,14 @@
         [result[:, :cut].reshape(n, ROWS, cut), rest.reshape(n, ROWS, cut)], axis=1
     ).astype(BF16)
 
-    def h_copy(i):
-        return pltpu.make_async_remote_copy(
-            src_ref=h_send.at[i],
-            dst_ref=h_recv.at[p],
-            send_sem=h_ss.at[i],
-            recv_sem=h_rs.at[p],
-            device_id=(c, lax.rem(p + i, n)),
-            device_id_type=MESH,
-        )
-
-    start_all(h_copy)
+    for k in range(n - 1):
+        i = n // 2 + (k + 1) // 2 * (1 if k % 2 else -1)
+        d = lax.rem(p + i, n)
+        go(h_send.at[i], h_recv.at[p], h_ss.at[i], h_rs.at[p], c, d)
 
     def h_add(i, total):
         s = lax.rem(p + i, n)
-        arrived(h_recv, h_rs, s)
+        arrived(h_recv.at[s], h_rs.at[s])
         return total + h_recv[s].astype(F32)
 
     summed = lax.fori_loop(1, n, h_add, h_send[0].astype(F32))
@@ -468,13 +554,14 @@
         [summed[:ROWS], summed[ROWS:, : columns - cut]], axis=1
     ).astype(BF16)
 
-    for make in (a_copy, c_copy, e_copy, l_copy, g_copy, h_copy):
-        finish_sends(make)
+    for copy in sent:
+        copy.wait_send()
 
     @pl.when(c != 0)
     def _():
-        b_remote().wait_send()
-        f_remote().wait_send()
+        b_copy(0).wait_send()
+        b_copy(1).wait_send()
+        f_copy().wait_send()
 
 
 def on_device(
@@ -501,8 +588,8 @@
     smem = pl.BlockSpec(memory_space=pltpu.SMEM)
     vmem = pl.BlockSpec(memory_space=pltpu.VMEM)
     hbm = pl.BlockSpec(memory_space=pl.ANY)
-    many = pltpu.SemaphoreType.DMA((n,))
-    two = pltpu.SemaphoreType.DMA((2,))
+    dma = pltpu.SemaphoreType.DMA
+    half_rows = own // 2 * (KVR // LANES) + own // 4
     return pl.pallas_call(
         functools.partial(kernel, n),
         out_shape=jax.ShapeDtypeStruct((ROWS, out_columns), BF16),
@@ -520,33 +607,41 @@
             pltpu.VMEM((n, 2 * ROWS, columns // 2), BF16),
             pltpu.VMEM((n, 2 * ROWS, columns // 2), BF16),
             pltpu.VMEM((KVR // LANES + 1, own, LANES), F32),
-            pltpu.VMEM((own, QK), BF16),
-            pltpu.VMEM((n, own, QK), BF16),
-            pltpu.VMEM((n, own, KVR), BF16),
-            pltpu.VMEM((ROWS, heads), F32),
-            pltpu.VMEM((n, own, KVR), BF16),
-            pltpu.VMEM((n, ROWS, heads), F32),
+            pltpu.VMEM((2, half_rows, LANES), BF16),
+            pltpu.VMEM((n, 2, half_rows, LANES), BF16),
+            pltpu.VMEM((SIDE, SIDE, own, KVR), BF16),
+            pltpu.VMEM((2, SIDE, SIDE, own // 2, KVR), BF16),
+            pltpu.VMEM((2, SIDE, own // 2, KVR), BF16),
+            pltpu.VMEM((2, SIDE, own // 2, KVR), BF16),
+            pltpu.VMEM((2, ROWS // 2, heads), F32),
+            pltpu.VMEM((2, SIDE, ROWS // 2, heads), F32),
+            pltpu.VMEM((2, SIDE, ROWS // 2, heads), F32),
+            pltpu.VMEM((2, ROWS // 2, heads), F32),
+            pltpu.VMEM((2, SIDE, ROWS // 2, heads), F32),
             pltpu.VMEM((own, KVR), BF16),
             pltpu.VMEM((own, KVR), BF16),
             pltpu.VMEM((KVR // LANES, own, LANES), F32),
             pltpu.VMEM((n, 2 * ROWS, HEADS // 2 * NOPE), BF16),
             pltpu.VMEM((n, 2 * ROWS, 256), BF16),
             pltpu.VMEM((n, 2 * ROWS, 256), BF16),
-            pltpu.SemaphoreType.DMA((6,)),
-            many,
-            many,
-            two,
-            many,
-            many,
-            many,
-            many,
-            many,
-            many,
-            two,
-            many,
-            many,
-            many,
-            many,
+            dma((6,)),
+            dma((n,)),
+            dma((n,)),
+            dma((2,)),
+            dma((2,)),
+            dma((30,)),
+            dma((n, 2)),
+            dma((24,)),
+            dma((2, SIDE, SIDE)),
+            dma((6,)),
+            dma((2, SIDE)),
+            dma((12,)),
+            dma((2, 2, SIDE)),
+            dma((2,)),
+            dma((n,)),
+            dma((n,)),
+            dma((n,)),
+            dma((n,)),
         ],
         compiler_params=pltpu.CompilerParams(
             collective_id=0, has_side_effects=True, vmem_limit_bytes=56 * 2**20

time: 83.5 us -> 69.7 us (0.83)
  Pallas kernels: 82 us -> 68.2 us
    pallas_call x1, Pallas kernels: 82 us -> 68.2 us  [on_device(): pl.pallas_call(functools.partial(kernel, n), out_shape=jax.ShapeDtypeStru...]
where the time goes in v2:
time: 69.7 us; the launch traced here: 69.5 us
  Pallas kernels  68.2 us (98%)
  local copies, waits for them, and re-layouts  1.3 us (2%)
    pallas_call x1, Pallas kernels, on_device(): pl.pallas_call(functools.partial(kernel, n), out_shape=jax.ShapeDtypeStru...  68.2 us

profile of v2, /device:TPU:1, one launch (start us, length us, event | category | flops | bytes accessed | tf_op | source)
XLA Modules:
  0.0 69.5 jit_solution(6079901291462978927)
XLA Ops:
  0.0 68.2 %shard_map.100 = bf16[8,448]{1,0:T(8,128)(2,1)} custom-call(s32[128]{0:T(128)} %lens.1, s32[8,32]{1,0:T(8,128)} %ids.1, s32[8]{0:T(128)} %counts.1, bf16[128,1536]{1,0:T(8,128)(2,1)} %cq_hbm.1, f32[12,128]{1,0:T(8,128)} %bitcast.5, bf16[96,1536]{1,0:T(8,128)(2,1)} %wq_hbm.1, bf16[8,128,512]{2,1,0:T(8,128)(2,1)} %wk_hbm.1, bf16[8,512,128]{2,1,0:T(8,128)(2,1)} %vup_hbm.1, ...), custom_call_target="tpu_custom_call" | custom-call | tf_op jit(solution)/shard_map/pallas_call | solution.py:593
  68.2 1.3 %copy.12 = bf16[8,448]{1,0:T(8,128)(2,1)} copy(bf16[8,448]{1,0:T(8,128)(2,1)} %shard_map.100) | data formatting | bytes 14336

commit v3 on v2

v3 whole, which is shorter than its diff:
```python
import functools

import jax
import jax.numpy as jnp
from jax import lax
from jax.experimental import pallas as pl
from jax.experimental.pallas import tpu as pltpu
from jax.sharding import PartitionSpec as P

NOPE = 128
ROPE = 64
KVR = 512
QK = KVR + ROPE
HEAD = NOPE + ROPE
BLK = 64
SLOTS = 4
ROWS = 8
HEADS = 8
LANES = 128
SIDE = 4
RING = (1, 3, 2)
FAR_FIRST = sorted(
    [(i, j) for i in range(SIDE) for j in range(SIDE) if i or j],
    key=lambda at: -min(at[0], SIDE - at[0]) - min(at[1], SIDE - at[1]),
)
MESH = pl.DeviceIdType.MESH
F32 = jnp.float32
BF16 = jnp.bfloat16


def kernel(
    n,
    lens,
    ids,
    counts,
    cq_hbm,
    gain,
    wq_hbm,
    wk_hbm,
    vup_hbm,
    wo_hbm,
    cache_hbm,
    out,
    cq,
    wq,
    wk,
    vup,
    wo,
    cache,
    keys,
    tokens_at,
    a_pair,
    a_send,
    a_recv,
    q_rows,
    b_send,
    q_all,
    o_send,
    o_first,
    o_merged,
    o_second,
    o_kept,
    l_send,
    l_first,
    l_first_share,
    l_second_share,
    l_next,
    l_second,
    f_send,
    f_recv,
    f_rows,
    v_all,
    h_send,
    h_recv,
    local_sem,
    a_ss,
    a_rs,
    b_ss,
    b_rs,
    c_ss,
    c_rs,
    e_ss,
    e_rs,
    l_ss,
    l_rs,
    f_ss,
    f_rs,
    g_sem,
    h_sem,
):
    c = lax.axis_index("cache")
    p = lax.axis_index("proj")
    x, y = c // SIDE, lax.rem(c, SIDE)

    def on_x(i):
        return lax.rem(x + i, SIDE) * SIDE + y

    def on_y(i):
        return x * SIDE + lax.rem(y + i, SIDE)

    def on_plane(k):
        dx, dy = FAR_FIRST[k]
        return lax.rem(x + dx, SIDE) * SIDE + lax.rem(y + dy, SIDE)

    def send(src, dst, send_sem, recv_sem, cache_at, proj_at):
        return pltpu.make_async_remote_copy(
            src_ref=src,
            dst_ref=dst,
            send_sem=send_sem,
            recv_sem=recv_sem,
            device_id=(cache_at, proj_at),
            device_id_type=MESH,
        )

    def arrived(ref, sem):
        pltpu.make_async_copy(ref, ref, sem).wait()

    def go(*copy):
        send(*copy).start()

    barrier = pltpu.get_barrier_semaphore()

    def greet(i, carry):
        pl.semaphore_signal(
            barrier, inc=1, device_id=(lax.rem(c + i, n), p), device_id_type=MESH
        )
        pl.semaphore_signal(
            barrier, inc=1, device_id=(c, lax.rem(p + i, n)), device_id_type=MESH
        )
        return carry

    lax.fori_loop(1, n, greet, 0)

    depth = wq_hbm.shape[0]
    width = cq.shape[1]
    span = wq.shape[0]
    start = jnp.minimum((c * depth) // 128 * 128, width - span)
    inside = c * depth - start
    wq[...] = jnp.zeros_like(wq)
    loads = [
        pltpu.make_async_copy(cq_hbm, cq, local_sem.at[0]),
        pltpu.make_async_copy(
            wq_hbm, wq.at[pl.ds(pl.multiple_of(inside, 32), depth)], local_sem.at[1]
        ),
        pltpu.make_async_copy(wk_hbm, wk, local_sem.at[2]),
        pltpu.make_async_copy(cache_hbm, cache, local_sem.at[3]),
        pltpu.make_async_copy(vup_hbm, vup, local_sem.at[4]),
        pltpu.make_async_copy(wo_hbm, wo, local_sem.at[5]),
    ]
    for load in loads:
        load.start()

    loads[0].wait()
    source = cq[...].astype(F32)
    norm = lax.rsqrt(jnp.mean(source * source, -1, keepdims=True) + 1e-06)
    share = pl.ds(pl.multiple_of(start, 128), span)
    tiles = [gain[pl.ds(start // LANES + t, 1), :] for t in range(span // LANES)]
    normed = (cq[:, share].astype(F32) * norm * jnp.concatenate(tiles, 1)).astype(BF16)
    loads[1].wait()
    turned_rows = pltpu.roll(normed.astype(F32).reshape(n, ROWS, span), ROWS // 2, 1)
    turned_rows = turned_rows.reshape(normed.shape).astype(BF16)
    quarter = a_send.shape[3]
    upper = lax.broadcasted_iota(jnp.int32, (n, ROWS, quarter), 1) < ROWS // 2
    for k in range(2):
        even = jnp.dot(
            normed, wq[:, 2 * k * quarter : (2 * k + 1) * quarter], preferred_element_type=F32
        ).reshape(n, ROWS, quarter)
        odd = jnp.dot(
            turned_rows,
            wq[:, (2 * k + 1) * quarter : (2 * k + 2) * quarter],
            preferred_element_type=F32,
        ).reshape(n, ROWS, quarter)
        a_pair[0, k] = jnp.where(upper, even, odd)
        a_pair[1, k] = jnp.where(upper, odd, even)
    for w in range(2):
        a_send[w] = jnp.concatenate([a_pair[w, 0], a_pair[w, 1]], axis=1).astype(BF16)

    pl.semaphore_wait(barrier, 2 * (n - 1))

    for w in range(2):
        for k in range(n - 1):
            d = on_plane(k)
            go(
                a_send.at[w, lax.rem(d + n - p, n)], a_recv.at[w, c], a_ss.at[w], a_rs.at[w], d, p
            )

    ctx_local = cache.shape[2]
    per_shard = ctx_local // BLK
    slots = ids.shape[1]
    tokens = SLOTS * BLK

    def column(ref, base, count=ROWS, repeats=1):
        rows = lax.broadcasted_iota(jnp.int32, (count * repeats, 1), 0)
        found = jnp.zeros((count * repeats, 1), jnp.int32)
        for r in range(count):
            found = jnp.where(rows % count == r, ref[base + r], found)
        return found

    local = ids[...] - c * per_shard
    slot = lax.broadcasted_iota(jnp.int32, (ROWS, slots), 1)
    mine = (slot < column(counts, 0)) & (local >= 0) & (local < per_shard)
    before = lax.broadcasted_iota(jnp.int32, (slots, slots), 0) < lax.broadcasted_iota(
        jnp.int32, (slots, slots), 1
    )
    order = jnp.dot(
        mine.astype(F32), before.astype(F32), preferred_element_type=F32
    )
    lane = lax.broadcasted_iota(jnp.int32, (ROWS, tokens), 1)
    picked = jnp.full((ROWS, tokens), -1, jnp.int32)
    for k in range(SLOTS):
        kept = mine & (order == float(k))
        found = jnp.sum(jnp.where(kept, local + 1, 0), -1, keepdims=True) - 1
        picked = jnp.where(lane // BLK == k, found, picked)
    at = picked * BLK + lane % BLK
    live_at = (picked >= 0) & (c * ctx_local + at < column(lens, p * ROWS))
    tokens_at[...] = jnp.where(live_at, at, -1)

    loads[3].wait()

    def gather(r, carry):
        chosen = lax.broadcasted_iota(jnp.int32, (ctx_local, tokens), 0) == tokens_at[
            pl.ds(r, 1), :
        ]
        keys[r] = jnp.dot(
            cache[r], chosen.astype(F32).astype(BF16), preferred_element_type=F32
        ).astype(BF16)
        return carry

    lax.fori_loop(0, ROWS, gather, 0)

    block = lax.rem(c + n - p, n)
    home = block == p

    others = pl.ds(0, n - 1)
    half_rope = ROPE // 2
    index = lax.broadcasted_iota(jnp.int32, (1, half_rope), 1)
    freq = jnp.zeros((1, half_rope), F32)
    for i in range(half_rope):
        freq = jnp.where(index == i, float(10000.0 ** (-2.0 * i / ROPE)), freq)
    four = ROWS // 2
    cosine, sine = [], []
    for w in range(2):
        angles = (column(lens, block * ROWS + w * four, four, 4) - 1).astype(F32) * freq
        cosine.append(jnp.cos(angles))
        sine.append(jnp.sin(angles))
    loads[2].wait()
    own = ROWS * HEADS
    part = own // 4
    latent_tiles = KVR // LANES
    blank = jnp.zeros((2 * ROWS, LANES - ROPE), F32)

    units = ROWS // 2
    roped = ((0, 0), (2, 1))
    sizes = [[3 * part if (m, k) in roped else 2 * part for k in range(2)] for m in range(units)]
    starts = [[sum(sum(size) for size in sizes[:m]) + sizes[m][0] * k for k in range(2)] for m in range(units)]

    def unit_rows(m):
        return pl.ds(starts[m][0], sum(sizes[m]))

    def half_of(m, k):
        return pl.ds(starts[m][k], sizes[m][k])

    def rope_rows(w):
        m, k = roped[w]
        return slice(starts[m][k] + 2 * part, starts[m][k] + 3 * part)

    def b_copy(m):
        rows = unit_rows(m)
        return send(b_send.at[rows], q_all.at[c, rows], b_ss.at[m], b_rs.at[m], c, block)

    for w in range(2):

        def add(i, total):
            return total + a_recv[w, lax.rem(c + i, n)].astype(F32)

        arrived(a_recv.at[w, others], a_rs.at[w])
        query = lax.fori_loop(1, n, add, a_send[w, block].astype(F32))
        for u in range(2):
            base = u * HEAD
            nope = query[:, base : base + NOPE].astype(BF16)
            first = query[:, base + NOPE : base + NOPE + half_rope]
            second = query[:, base + NOPE + half_rope : base + HEAD]
            turned = jnp.concatenate(
                [
                    first * cosine[w] - second * sine[w],
                    first * sine[w] + second * cosine[w],
                    blank,
                ],
                axis=1,
            )
            for k in range(4):
                h = 2 * (k ^ w) + u
                here = slice(k * four, (k + 1) * four)
                latent = jnp.dot(nope, wk[h], preferred_element_type=F32)[here]
                place = pl.ds(h, four, stride=HEADS)
                for t in range(latent_tiles):
                    q_rows[w, t, place, :] = latent[:, t * LANES : (t + 1) * LANES]
                q_rows[w, latent_tiles, place, :] = turned[here]
        for u in range(2):
            rows = slice(u * part, (u + 1) * part)
            for t in range(latent_tiles):
                at = starts[2 * w + u][t // 2] + t % 2 * part
                b_send[at : at + part, :] = q_rows[w, t, rows, :].astype(BF16)
        ropes = [
            q_rows[w, latent_tiles, u * part : (u + 1) * part, :][:, :ROPE] for u in range(2)
        ]
        b_send[rope_rows(w), :] = jnp.concatenate(ropes, axis=1).astype(BF16)

        @pl.when(jnp.logical_not(home))
        def _():
            b_copy(2 * w).start()
            b_copy(2 * w + 1).start()

    @pl.when(home)
    def _():
        q_all[c] = b_send[...]

    along = (on_x, on_y)

    def spread(s, m, k, to, sem):
        ref = q_all.at[s, half_of(m, k)]
        go(ref, ref, c_ss.at[0], sem, to, p)

    for m in range(units):

        @pl.when(jnp.logical_not(home))
        def _():
            b_copy(m).wait_recv()

        for i in RING:
            for k in range(2):
                spread(c, m, k, along[k](i), c_rs.at[m, k, SIDE - i])
        for i in RING:
            for k in range(2):
                spread(c, m, k, along[1 - k](i), c_rs.at[m, k, 0])
    for m in range(units):
        for i in RING:
            for k in range(2):
                s = along[k](i)
                arrived(q_all.at[s, half_of(m, k)], c_rs.at[m, k, i])
                for j in RING:
                    spread(s, m, k, along[1 - k](j), c_rs.at[m, k, 0])

    def all_arrived(m):
        for k in range(2):
            arrived(q_all.at[pl.ds(0, SIDE * (SIDE - 1)), half_of(m, k)], c_rs.at[m, k, 0])

    scale = HEAD ** (-0.5)
    heads = n * HEADS
    eye = lax.broadcasted_iota(jnp.int32, (heads, heads), 0) == lax.broadcasted_iota(
        jnp.int32, (heads, heads), 1
    )

    def attend(r, q):
        live = tokens_at[r : r + 1, :] >= 0
        key = keys[r]
        scores = jnp.dot(q, key, preferred_element_type=F32) * scale
        largest = jnp.max(jnp.where(live, scores, -1e30), -1, keepdims=True)
        weights = jnp.where(live, jnp.exp(scores - largest), 0.0)
        total = jnp.sum(weights, -1, keepdims=True)
        summed = lax.dot_general(
            weights.astype(BF16),
            key[:KVR],
            (((1,), (1,)), ((), ())),
            preferred_element_type=F32,
        )
        some = total > 0.0
        safe = jnp.where(some, total, 1.0)
        logs = jnp.where(some, largest + jnp.log(safe), -1e30)
        l_send[r // 2, r % 2 : r % 2 + 1, :] = jnp.sum(jnp.where(eye, logs, 0.0), 0, keepdims=True)
        return summed * (1.0 / safe)

    def pair(m):
        tiles = []
        for t in range(latent_tiles):
            at = starts[m][t // 2] + t % 2 * part
            tiles.append(q_all[:, at : at + part, :])
        tiles.append(q_all[:, rope_rows(m // 2), m % 2 * ROPE : (m % 2 + 1) * ROPE])
        q = jnp.concatenate([tile.astype(F32) for tile in tiles], axis=2)
        first = attend(2 * m, q[:, :HEADS, :].reshape(heads, QK).astype(BF16))
        second = attend(2 * m + 1, q[:, HEADS:, :].reshape(heads, QK).astype(BF16))
        both = jnp.concatenate(
            [first.reshape(n, HEADS, KVR), second.reshape(n, HEADS, KVR)], axis=1
        ).astype(BF16)
        o_send[m] = both.reshape(SIDE, SIDE, part, KVR)

    half_lanes = KVR // 2

    def lanes(k):
        return pl.ds(k * half_lanes, half_lanes)

    def place_of(k, first, second):
        return (first, second) if k == 0 else (second, first)

    me = (x, y)
    three = pl.ds(0, SIDE - 1)

    def slot_of(v, i):
        return lax.rem(v + i, SIDE)

    def send_logs(src, dst, k, m, stage, axis):
        for i in RING:
            go(src, dst.at[k, m, me[axis]], l_ss.at[stage], l_rs.at[k, m, stage], along[axis](i), p)

    def first_stage(m):
        for k in range(2):
            l_first[k, m, me[k]] = l_send[m]
            send_logs(l_send.at[m], l_first, k, m, 0, k)
        for j in RING + (0,):
            for i in RING:
                for k in range(2):
                    to = slot_of(me[1 - k], j)
                    at = place_of(k, slot_of(me[k], i), to)
                    go(
                        o_send.at[m, at[0], at[1], :, lanes(k)],
                        o_first.at[k, m, me[k], to],
                        e_ss.at[0],
                        e_rs.at[k, m, to],
                        along[k](i),
                        p,
                    )

    spot = lax.broadcasted_iota(jnp.int32, (part, heads), 1) - (
        lax.broadcasted_iota(jnp.int32, (part, heads), 0) % HEADS
    )

    def share_column(share, d):
        wide = jnp.broadcast_to(share[:, None, :], (2, HEADS, heads)).reshape(part, heads)
        narrow = jnp.sum(jnp.where(spot == d * HEADS, wide, 0.0), -1, keepdims=True)
        return jnp.broadcast_to(narrow, (part, LANES))

    def scaled(value, share):
        return value.astype(F32) * jnp.concatenate([share] * (half_lanes // LANES), axis=1)

    def shares(buffer, k, m, stage):
        arrived(buffer.at[k, m, three], l_rs.at[k, m, stage])
        logs = buffer[k, m]
        top = jnp.max(logs, 0, keepdims=True)
        raised = jnp.exp(logs - top)
        total = jnp.sum(raised, 0, keepdims=True)
        return raised / total, (top + jnp.log(total))[0]

    def merge(k, m, to):
        at = place_of(k, me[k], to)
        total = scaled(o_send[m, at[0], at[1], :, lanes(k)], l_first_share[k, m, to, me[k]])
        arrived(o_first.at[k, m, three, to], e_rs.at[k, m, to])
        for i in RING:
            s = slot_of(me[k], i)
            total = total + scaled(o_first[k, m, s, to], l_first_share[k, m, to, s])
        return total

    def second_stage(m):
        for k in range(2):
            share, merged = shares(l_first, k, m, 0)
            l_next[k, m] = merged
            l_second[k, m, me[1 - k]] = merged
            send_logs(l_next.at[k, m], l_second, k, m, 1, 1 - k)
            for to in range(SIDE):
                at = place_of(k, me[k], to)
                for s in range(SIDE):
                    l_first_share[k, m, to, s] = share_column(share[s], at[0] * SIDE + at[1])
        for j in RING:
            for k in range(2):
                to = slot_of(me[1 - k], j)
                o_merged[k, m, to] = merge(k, m, to).astype(BF16)
                go(
                    o_merged.at[k, m, to],
                    o_second.at[k, m, me[1 - k]],
                    e_ss.at[1],
                    e_rs.at[k, m, SIDE],
                    along[1 - k](j),
                    p,
                )
        for k in range(2):
            o_kept[k, m] = merge(k, m, me[1 - k])

    def finish(m):
        for k in range(2):
            share, _ = shares(l_second, k, m, 1)
            for s in range(SIDE):
                l_second_share[k, m, s] = share_column(share[s], c)
        for k in range(2):
            total = scaled(o_kept[k, m], l_second_share[k, m, me[1 - k]])
            arrived(o_second.at[k, m, three], e_rs.at[k, m, SIDE])
            for i in RING:
                s = slot_of(me[1 - k], i)
                total = total + scaled(o_second[k, m, s], l_second_share[k, m, s])
            f_send[m, :, lanes(k)] = total.astype(BF16)

    def attention(m):
        all_arrived(m)
        pair(m)
        first_stage(m)

    for m in range(units):
        attention(m)
    for m in range(units):
        second_stage(m)

    def f_copy(w):
        two = pl.ds(2 * w, 2)
        return send(f_send.at[two], f_recv.at[two], f_ss.at[w], f_rs.at[w], c, block)

    for w in range(2):
        for m in (2 * w, 2 * w + 1):
            finish(m)

        @pl.when(jnp.logical_not(home))
        def _():
            f_copy(w).start()

    @pl.when(jnp.logical_not(home))
    def _():
        f_copy(0).wait_recv()
        f_copy(1).wait_recv()

    @pl.when(home)
    def _():
        f_recv[...] = f_send[...]

    per_half = HEADS // 2
    loads[4].wait()
    for m in range(units):
        for t in range(latent_tiles):
            f_rows[t, m * part : (m + 1) * part, :] = f_recv[
                m, :, t * LANES : (t + 1) * LANES
            ].astype(F32)
    values = [
        jnp.dot(
            jnp.concatenate(
                [f_rows[t, pl.ds(h, ROWS, stride=HEADS), :] for t in range(KVR // LANES)], 1
            ).astype(BF16),
            vup[h],
            preferred_element_type=F32,
        )
        for h in range(HEADS)
    ]
    v_all[c] = jnp.concatenate(
        [jnp.concatenate(values[:per_half], 1), jnp.concatenate(values[per_half:], 1)], 0
    ).astype(BF16)

    for k in range(n - 1):
        go(v_all.at[c], v_all.at[c], g_sem.at[0], g_sem.at[1], on_plane(k), p)
    loads[5].wait()
    arrived(v_all.at[others], g_sem.at[1])

    v = v_all[...].astype(F32)
    wide = v.shape[2]
    rows = n * ROWS
    low = v[:, :ROWS, :].reshape(rows, wide).astype(BF16)
    high = v[:, ROWS:, :].reshape(rows, wide).astype(BF16)
    across = (((1,), (1,)), ((), ()))
    result = lax.dot_general(
        low, wo[:, :wide], across, preferred_element_type=F32
    ) + lax.dot_general(high, wo[:, wide:], across, preferred_element_type=F32)
    columns = wo.shape[0]
    cut = h_send.shape[2]
    rest = jnp.concatenate(
        [result[:, cut:], jnp.zeros((rows, 2 * cut - columns), F32)], axis=1
    )
    h_send[...] = jnp.concatenate(
        [result[:, :cut].reshape(n, ROWS, cut), rest.reshape(n, ROWS, cut)], axis=1
    ).astype(BF16)

    own_slot = lax.rem(p + p, n)
    for k in range(n - 1):
        i = n // 2 + (k + 1) // 2 * (1 if k % 2 else -1)
        d = lax.rem(p + i, n)
        go(h_send.at[lax.rem(d + p, n)], h_recv.at[p], h_sem.at[0], h_sem.at[1], c, d)

    def h_add(i, total):
        s = lax.rem(p + i, n)
        return total + h_recv[s].astype(F32)

    arrived(h_recv.at[others], h_sem.at[1])
    summed = lax.fori_loop(1, n, h_add, h_send[own_slot].astype(F32))
    out[...] = jnp.concatenate(
        [summed[:ROWS], summed[ROWS:, : columns - cut]], axis=1
    ).astype(BF16)

    for w in range(2):
        arrived(a_send.at[w, others], a_ss.at[w])
    arrived(q_all.at[others], c_ss.at[0])
    arrived(o_first.at[:, :, three], e_ss.at[0])
    arrived(o_merged.at[:, :, three], e_ss.at[1])
    arrived(l_first.at[:, :, three], l_ss.at[0])
    arrived(l_second.at[:, :, three], l_ss.at[1])
    arrived(v_all.at[others], g_sem.at[0])
    arrived(h_send.at[others], h_sem.at[0])

    @pl.when(jnp.logical_not(home))
    def _():
        for w in range(2):
            f_copy(w).wait_send()
        for m in range(units):
            b_copy(m).wait_send()


def on_device(
    compressed_query,
    query_gain,
    w_query,
    w_key,
    value_up_weight,
    w_output,
    latent_cache,
    context_lengths,
    block_ids,
    block_counts,
):
    n = lax.axis_size("cache")
    rows, rank = compressed_query.shape
    depth, columns = w_query.shape
    span = 256
    w_output = w_output.T
    latent_cache = latent_cache.transpose(0, 2, 1)
    heads = n * HEADS
    own = ROWS * HEADS
    out_columns = w_output.shape[0]
    smem = pl.BlockSpec(memory_space=pltpu.SMEM)
    vmem = pl.BlockSpec(memory_space=pltpu.VMEM)
    hbm = pl.BlockSpec(memory_space=pl.ANY)
    dma = pltpu.SemaphoreType.DMA
    units = ROWS // 2
    chunk = own * QK // LANES
    return pl.pallas_call(
        functools.partial(kernel, n),
        out_shape=jax.ShapeDtypeStruct((ROWS, out_columns), BF16),
        in_specs=[smem, vmem, smem, hbm, vmem, hbm, hbm, hbm, hbm, hbm],
        out_specs=vmem,
        scratch_shapes=[
            pltpu.VMEM((rows, rank), BF16),
            pltpu.VMEM((span, columns), BF16),
            pltpu.VMEM(w_key.shape, BF16),
            pltpu.VMEM(value_up_weight.shape, BF16),
            pltpu.VMEM(w_output.shape, BF16),
            pltpu.VMEM(latent_cache.shape, BF16),
            pltpu.VMEM((ROWS, QK, SLOTS * BLK), BF16),
            pltpu.VMEM((ROWS, SLOTS * BLK), jnp.int32),
            pltpu.VMEM((2, 2, n, ROWS, columns // 4), F32),
            pltpu.VMEM((2, n, 2 * ROWS, columns // 4), BF16),
            pltpu.VMEM((2, n, 2 * ROWS, columns // 4), BF16),
            pltpu.VMEM((2, KVR // LANES + 1, own // 2, LANES), F32),
            pltpu.VMEM((chunk, LANES), BF16),
            pltpu.VMEM((n, chunk, LANES), BF16),
            pltpu.VMEM((units, SIDE, SIDE, 2 * HEADS, KVR), BF16),
            pltpu.VMEM((2, units, SIDE, SIDE, 2 * HEADS, KVR // 2), BF16),
            pltpu.VMEM((2, units, SIDE, 2 * HEADS, KVR // 2), BF16),
            pltpu.VMEM((2, units, SIDE, 2 * HEADS, KVR // 2), BF16),
            pltpu.VMEM((2, units, 2 * HEADS, KVR // 2), F32),
            pltpu.VMEM((units, 2, heads), F32),
            pltpu.VMEM((2, units, SIDE, 2, heads), F32),
            pltpu.VMEM((2, units, SIDE, SIDE, 2 * HEADS, LANES), F32),
            pltpu.VMEM((2, units, SIDE, 2 * HEADS, LANES), F32),
            pltpu.VMEM((2, units, 2, heads), F32),
            pltpu.VMEM((2, units, SIDE, 2, heads), F32),
            pltpu.VMEM((units, 2 * HEADS, KVR), BF16),
            pltpu.VMEM((units, 2 * HEADS, KVR), BF16),
            pltpu.VMEM((KVR // LANES, own, LANES), F32),
            pltpu.VMEM((n, 2 * ROWS, HEADS // 2 * NOPE), BF16),
            pltpu.VMEM((n, 2 * ROWS, 256), BF16),
            pltpu.VMEM((n, 2 * ROWS, 256), BF16),
            dma((6,)),
            dma((2,)),
            dma((2,)),
            dma((units,)),
            dma((units,)),
            dma((1,)),
            dma((units, 2, SIDE)),
            dma((2,)),
            dma((2, units, SIDE + 1)),
            dma((2,)),
            dma((2, units, 2)),
            dma((2,)),
            dma((2,)),
            dma((2,)),
            dma((2,)),
        ],
        compiler_params=pltpu.CompilerParams(
            collective_id=0, has_side_effects=True, vmem_limit_bytes=56 * 2**20
        ),
    )(
        context_lengths,
        block_ids,
        block_counts,
        compressed_query,
        query_gain.reshape(rank // LANES, LANES),
        w_query,
        w_key,
        value_up_weight,
        w_output,
        latent_cache,
    )


def solution(mesh):
    placed = (
        P(),
        P(),
        P("cache", "proj"),
        P("proj", None, None),
        P("proj", None, None),
        P("proj", "cache"),
        P("proj", "cache", None),
        P(),
        P("proj", None),
        P("proj"),
    )
    return jax.shard_map(
        on_device, mesh=mesh, in_specs=placed, out_specs=P("proj", "cache"), check_vma=False
    )
```

time: 69.7 us -> 60.2 us (0.86)
  Pallas kernels: 68.2 us -> 58.7 us
    pallas_call x1, Pallas kernels: 68.2 us -> 58.7 us  [on_device(): pl.pallas_call(functools.partial(kernel, n), out_shape=jax.ShapeDtypeStru...]
where the time goes in v3:
time: 60.2 us; the launch traced here: 60 us
  Pallas kernels  58.7 us (98%)
  local copies, waits for them, and re-layouts  1.3 us (2%)
    pallas_call x1, Pallas kernels, on_device(): pl.pallas_call(functools.partial(kernel, n), out_shape=jax.ShapeDtypeStru...  58.7 us
    unnamed x1, local copies, waits for them, and re-layouts  1.3 us

profile of v3, /device:TPU:1, one launch (start us, length us, event | category | flops | bytes accessed | tf_op | source)
XLA Modules:
  0.0 60.0 jit_solution(9595233195003344434)
XLA Ops:
  0.0 58.7 %shard_map.100 = bf16[8,448]{1,0:T(8,128)(2,1)} custom-call(s32[128]{0:T(128)} %lens.1, s32[8,32]{1,0:T(8,128)} %ids.1, s32[8]{0:T(128)} %counts.1, bf16[128,1536]{1,0:T(8,128)(2,1)} %cq_hbm.1, f32[12,128]{1,0:T(8,128)} %bitcast.5, bf16[96,1536]{1,0:T(8,128)(2,1)} %wq_hbm.1, bf16[8,128,512]{2,1,0:T(8,128)(2,1)} %wk_hbm.1, bf16[8,512,128]{2,1,0:T(8,128)(2,1)} %vup_hbm.1, ...), custom_call_target="tpu_custom_call" | custom-call | tf_op jit(solution)/shard_map/pallas_call | solution.py:626
  58.7 1.3 %copy.12 = bf16[8,448]{1,0:T(8,128)(2,1)} copy(bf16[8,448]{1,0:T(8,128)(2,1)} %shard_map.100) | data formatting | bytes 14336

commit v4 on v3

--- a/solution.py
+++ b/solution.py
@@ -85,7 +85,8 @@
     l_rs,
     f_ss,
     f_rs,
-    g_sem,
+    g_ss,
+    g_rs,
     h_sem,
 ):
     c = lax.axis_index("cache")
@@ -497,62 +498,73 @@
     for m in range(units):
         second_stage(m)
 
-    def f_copy(w):
-        two = pl.ds(2 * w, 2)
-        return send(f_send.at[two], f_recv.at[two], f_ss.at[w], f_rs.at[w], c, block)
-
-    for w in range(2):
-        for m in (2 * w, 2 * w + 1):
-            finish(m)
+    def f_copy(m):
+        return send(f_send.at[m], f_recv.at[m], f_ss.at[m], f_rs.at[m], c, block)
+
+    for m in range(units):
+        finish(m)
 
         @pl.when(jnp.logical_not(home))
         def _():
-            f_copy(w).start()
-
-    @pl.when(jnp.logical_not(home))
-    def _():
-        f_copy(0).wait_recv()
-        f_copy(1).wait_recv()
+            f_copy(m).start()
 
     @pl.when(home)
     def _():
         f_recv[...] = f_send[...]
 
-    per_half = HEADS // 2
     loads[4].wait()
-    for m in range(units):
-        for t in range(latent_tiles):
-            f_rows[t, m * part : (m + 1) * part, :] = f_recv[
-                m, :, t * LANES : (t + 1) * LANES
-            ].astype(F32)
-    values = [
-        jnp.dot(
-            jnp.concatenate(
-                [f_rows[t, pl.ds(h, ROWS, stride=HEADS), :] for t in range(KVR // LANES)], 1
-            ).astype(BF16),
-            vup[h],
+    for w in range(2):
+
+        @pl.when(jnp.logical_not(home))
+        def _():
+            f_copy(2 * w).wait_recv()
+            f_copy(2 * w + 1).wait_recv()
+
+        for u in range(2):
+            for t in range(latent_tiles):
+                f_rows[w, t, u * part : (u + 1) * part, :] = f_recv[
+                    2 * w + u, :, t * LANES : (t + 1) * LANES
+                ].astype(F32)
+        values = []
+        for h in range(HEADS):
+            row_tiles = [
+                f_rows[w, t, pl.ds(h, four, stride=HEADS), :] for t in range(latent_tiles)
+            ]
+            values.append(
+                jnp.dot(
+                    jnp.concatenate(row_tiles, 1).astype(BF16),
+                    vup[h],
+                    preferred_element_type=F32,
+                )
+            )
+        quarters = [
+            jnp.concatenate([values[2 * (k ^ w)], values[2 * (k ^ w) + 1]], 1) for k in range(4)
+        ]
+        v_all[w, c] = jnp.concatenate(quarters, 0).astype(BF16)
+        for k in range(n - 1):
+            go(v_all.at[w, c], v_all.at[w, c], g_ss.at[w], g_rs.at[w], on_plane(k), p)
+    loads[5].wait()
+    for w in range(2):
+        arrived(v_all.at[w, others], g_rs.at[w])
+
+    wide = v_all.shape[3]
+    rows = n * ROWS
+    above = lax.broadcasted_iota(jnp.int32, (n, ROWS, wide), 1) < four
+    across = (((1,), (1,)), ((), ()))
+    result = None
+    for k in range(2):
+        early = v_all[0, :, k * ROWS : (k + 1) * ROWS, :].astype(F32)
+        late = v_all[1, :, k * ROWS : (k + 1) * ROWS, :].astype(F32)
+        even = jnp.where(above, early, late)
+        odd = pltpu.roll(jnp.where(above, late, early), four, 1)
+        both = jnp.concatenate([even.reshape(rows, wide), odd.reshape(rows, wide)], 1).astype(BF16)
+        term = lax.dot_general(
+            both,
+            wo[:, 2 * k * wide : 2 * (k + 1) * wide],
+            across,
             preferred_element_type=F32,
         )
-        for h in range(HEADS)
-    ]
-    v_all[c] = jnp.concatenate(
-        [jnp.concatenate(values[:per_half], 1), jnp.concatenate(values[per_half:], 1)], 0
-    ).astype(BF16)
-
-    for k in range(n - 1):
-        go(v_all.at[c], v_all.at[c], g_sem.at[0], g_sem.at[1], on_plane(k), p)
-    loads[5].wait()
-    arrived(v_all.at[others], g_sem.at[1])
-
-    v = v_all[...].astype(F32)
-    wide = v.shape[2]
-    rows = n * ROWS
-    low = v[:, :ROWS, :].reshape(rows, wide).astype(BF16)
-    high = v[:, ROWS:, :].reshape(rows, wide).astype(BF16)
-    across = (((1,), (1,)), ((), ()))
-    result = lax.dot_general(
-        low, wo[:, :wide], across, preferred_element_type=F32
-    ) + lax.dot_general(high, wo[:, wide:], across, preferred_element_type=F32)
+        result = term if result is None else result + term
     columns = wo.shape[0]
     cut = h_send.shape[2]
     rest = jnp.concatenate(
@@ -585,15 +597,15 @@
     arrived(o_merged.at[:, :, three], e_ss.at[1])
     arrived(l_first.at[:, :, three], l_ss.at[0])
     arrived(l_second.at[:, :, three], l_ss.at[1])
-    arrived(v_all.at[others], g_sem.at[0])
+    for w in range(2):
+        arrived(v_all.at[w, others], g_ss.at[w])
     arrived(h_send.at[others], h_sem.at[0])
 
     @pl.when(jnp.logical_not(home))
     def _():
-        for w in range(2):
-            f_copy(w).wait_send()
         for m in range(units):
             b_copy(m).wait_send()
+            f_copy(m).wait_send()
 
 
 def on_device(
@@ -656,8 +668,8 @@
             pltpu.VMEM((2, units, SIDE, 2, heads), F32),
             pltpu.VMEM((units, 2 * HEADS, KVR), BF16),
             pltpu.VMEM((units, 2 * HEADS, KVR), BF16),
-            pltpu.VMEM((KVR // LANES, own, LANES), F32),
-            pltpu.VMEM((n, 2 * ROWS, HEADS // 2 * NOPE), BF16),
+            pltpu.VMEM((2, KVR // LANES, own // 2, LANES), F32),
+            pltpu.VMEM((2, n, 2 * ROWS, HEADS // 4 * NOPE), BF16),
             pltpu.VMEM((n, 2 * ROWS, 256), BF16),
             pltpu.VMEM((n, 2 * ROWS, 256), BF16),
             dma((6,)),
@@ -671,7 +683,8 @@
             dma((2, units, SIDE + 1)),
             dma((2,)),
             dma((2, units, 2)),
-            dma((2,)),
+            dma((units,)),
+            dma((units,)),
             dma((2,)),
             dma((2,)),
             dma((2,)),

time: 60.2 us -> 59.9 us (level)
  no operation moved by 1% of the time
where the time goes in v4:
time: 59.9 us; the launch traced here: 59.7 us
  Pallas kernels  58.4 us (97%)
  local copies, waits for them, and re-layouts  1.3 us (2%)
    pallas_call x1, Pallas kernels, on_device(): pl.pallas_call(functools.partial(kernel, n), out_shape=jax.ShapeDtypeStru...  58.4 us
    unnamed x1, local copies, waits for them, and re-layouts  1.3 us

profile of v4, /device:TPU:1, one launch (start us, length us, event | category | flops | bytes accessed | tf_op | source)
XLA Modules:
  0.0 59.7 jit_solution(7596685795601115170)
XLA Ops:
  0.0 58.4 %shard_map.100 = bf16[8,448]{1,0:T(8,128)(2,1)} custom-call(s32[128]{0:T(128)} %lens.1, s32[8,32]{1,0:T(8,128)} %ids.1, s32[8]{0:T(128)} %counts.1, bf16[128,1536]{1,0:T(8,128)(2,1)} %cq_hbm.1, f32[12,128]{1,0:T(8,128)} %bitcast.5, bf16[96,1536]{1,0:T(8,128)(2,1)} %wq_hbm.1, bf16[8,128,512]{2,1,0:T(8,128)(2,1)} %wk_hbm.1, bf16[8,512,128]{2,1,0:T(8,128)(2,1)} %vup_hbm.1, ...), custom_call_target="tpu_custom_call" | custom-call | tf_op jit(solution)/shard_map/pallas_call | solution.py:638
  58.4 1.3 %copy.12 = bf16[8,448]{1,0:T(8,128)(2,1)} copy(bf16[8,448]{1,0:T(8,128)(2,1)} %shard_map.100) | data formatting | bytes 14336
